TPU v7x, 256 devices: a whole 4x4x8 slice. The times are simulated.
256 devices in a mesh: grp: 4 (over x), tp: 8 (over z), mem: 8 (over y, core).
Axes of the slice: x: 4, y: 4, z: 8, core: 2. Of those that a mesh axis runs over, the one named last changes fastest.
Arguments:
- tokens: bfloat16 [64, 12288], P('grp', 'mem'), may hold values from -110 to 110, as said below
- norm_gain: float32 [12288], P('mem'), may hold values from 0.5 to 1.5
- w_query: bfloat16 [12288, 12288], P('mem', 'tp'), may hold values from -0.0546875 to 0.0546875
- w_keyval: bfloat16 [2, 12288, 1024], P(None, 'mem', 'tp'), may hold values from -0.0546875 to 0.0546875
- w_out: bfloat16 [12288, 12288], P('tp', 'mem'), may hold values from -0.25 to 0.25
- key_cache: bfloat16 [8, 1024, 128, 128], P('tp', ('grp', 'mem')), may hold values from -1000 to 1000, as said below
- value_cache: bfloat16 [8, 1024, 128, 128], P('tp', ('grp', 'mem')), may hold values from -6 to 6
- req_len: int32 [64], replicated, may hold values from 1 to 2047, as said below
- span_request: int32 [1024], P(('grp', 'mem')), may hold values from -1 to 63, as said below
- span_first: int32 [1024], P(('grp', 'mem')), may hold values from 0 to 1920, as said below
- new_slot: int32 [64], replicated, may hold values from 0 to 1023, as said below
Outputs:
- attn_out: bfloat16 [64, 12288], P('grp', 'mem')
Inputs may be any that keep to these rules, and one draw needn't show every extreme that they name: Every request holds ceil((req_len + 1) / 128) spans with firsts 0, 128, 256, ...; at most 16 spans a request; one request has exactly 16 spans. `span_request`: each request's spans sit in distinct slots; on every owner the used slots come first, then empty ones (-1); owners are filled unevenly. `span_first`: multiple of 128; 0 in empty slots. `new_slot`: the slot of the request's span that contains position req_len. `tokens`: real values. `key_cache`: real values.
All inputs are finite; a program needn't handle non-finite values.
Results may differ from a plain program's by a relative error of at most 0.015.
Values may be sent and summed in bfloat16 or wider, within the bound.
A program may use at most 64 MiB of HBM per device.

v0:
```python
import jax
import jax.numpy as jnp
from jax import lax
from jax.sharding import PartitionSpec as P

D = 12288


epsilon = 1e-05
rope_base = 1000000.0
very_low = -1e30


def joined(value, axis, combine):
    everything = jax.tree.map(lambda part: lax.all_gather(part, axis), value)
    first = jax.tree.map(lambda part: part[0], everything)

    def step(k, so_far):
        return combine(so_far, jax.tree.map(lambda part: part[k], everything))

    return lax.fori_loop(1, lax.axis_size(axis), step, first)


def rotary(vectors, positions):
    halfway = vectors.shape[-1] // 2
    frequency = rope_base ** (-(jnp.arange(halfway).astype(jnp.float32) * 2.0) / vectors.shape[-1])
    angles = positions.astype(jnp.float32)[:, None] * frequency[None, :]
    c = jnp.cos(angles)[:, None, :]
    s = jnp.sin(angles)[:, None, :]
    a = vectors[..., :halfway]
    b = vectors[..., halfway:]
    return jnp.concatenate([a * c - b * s, a * s + b * c], axis=-1)


def finish_rows(summed, square_sum, lengths, q_cols, kv_cols, head_dim):
    root_mean = jnp.sqrt(square_sum / D + epsilon)
    normed = summed / root_mean[:, None]
    row_count = normed.shape[0]
    query_part = rotary(
        normed[:, :q_cols].reshape(row_count, q_cols // head_dim, head_dim), lengths
    )
    key_part = rotary(
        normed[:, q_cols : q_cols + kv_cols].reshape(row_count, kv_cols // head_dim, head_dim),
        lengths,
    )
    value_part = normed[:, q_cols + kv_cols :]
    return jnp.concatenate(
        [query_part.reshape(row_count, q_cols), key_part.reshape(row_count, kv_cols), value_part],
        axis=1,
    ).astype(jnp.bfloat16)


def blend(first_part, second_part):
    top = jnp.maximum(first_part[0], second_part[0])
    left = jnp.exp(first_part[0] - top)
    right = jnp.exp(second_part[0] - top)
    total = first_part[1] * left + second_part[1] * right
    accum = first_part[2] * left[..., None] + second_part[2] * right[..., None]
    return (top, total, accum)


def per_device(
    tokens,
    norm_gain,
    w_query,
    w_keyval,
    w_out,
    key_cache,
    value_cache,
    req_len,
    span_request,
    span_first,
    new_slot,
):
    head_dim = key_cache.shape[-1]
    kv_local = key_cache.shape[0]
    span_len = key_cache.shape[2]
    q_cols = w_query.shape[1]
    kv_cols = w_keyval.shape[2]
    heads_local = q_cols // head_dim
    group_size = heads_local // kv_local
    rows_grp = tokens.shape[0]
    requests = req_len.shape[0]
    n_mem = lax.axis_size("mem")
    owner_index = lax.axis_index("grp") * n_mem + lax.axis_index("mem")
    tokens_wide = tokens.astype(jnp.float32)
    local_square = jnp.sum(tokens_wide * tokens_wide, axis=1)
    scaled = (tokens_wide * norm_gain[None, :]).astype(jnp.bfloat16)
    projected = jnp.concatenate(
        [
            jnp.dot(scaled, w_query, preferred_element_type=jnp.float32),
            jnp.dot(scaled, w_keyval[0], preferred_element_type=jnp.float32),
            jnp.dot(scaled, w_keyval[1], preferred_element_type=jnp.float32),
        ],
        axis=1,
    )
    summed, square_sum = lax.psum((projected, local_square), "mem")
    first_row = lax.axis_index("grp") * rows_grp
    lengths = lax.dynamic_slice_in_dim(req_len, first_row, rows_grp, 0)
    own_rows = finish_rows(summed, square_sum, lengths, q_cols, kv_cols, head_dim)
    everything = lax.all_gather(own_rows, "grp", axis=0, tiled=True)
    queries = everything[:, :q_cols].reshape(requests, kv_local, group_size, head_dim)
    new_keys = everything[:, q_cols : q_cols + kv_cols].reshape(requests, kv_local, head_dim)
    new_values = everything[:, q_cols + kv_cols :].reshape(requests, kv_local, head_dim)
    slot_count = span_request.shape[0]
    block_len = min(16, slot_count)
    live_count = jnp.sum((span_request >= 0).astype(jnp.int32))
    block_total = (live_count + block_len - 1) // block_len
    slot_base = owner_index * slot_count
    request_ids = jnp.arange(requests, dtype=jnp.int32)

    def advance(b, running):
        top, total, accum = running
        offset = b * block_len
        block_req = lax.dynamic_slice_in_dim(span_request, offset, block_len, 0)
        block_first = lax.dynamic_slice_in_dim(span_first, offset, block_len, 0)
        key_block = lax.dynamic_slice_in_dim(key_cache, offset, block_len, 1)
        value_block = lax.dynamic_slice_in_dim(value_cache, offset, block_len, 1)
        owner_req = jnp.maximum(block_req, 0)
        lengths_here = req_len[owner_req]
        positions = block_first[:, None] + jnp.arange(span_len, dtype=jnp.int32)[None, :]
        visible = (block_req >= 0)[:, None] & (positions <= lengths_here[:, None])
        slot_ids = slot_base + offset + jnp.arange(block_len, dtype=jnp.int32)
        brand_new = (
            visible
            & (positions == lengths_here[:, None])
            & (slot_ids == new_slot[owner_req])[:, None]
        )
        fresh_keys = new_keys[owner_req].transpose(1, 0, 2)[:, :, None, :]
        fresh_values = new_values[owner_req].transpose(1, 0, 2)[:, :, None, :]
        key_block = jnp.where(brand_new[None, :, :, None], fresh_keys, key_block)
        value_block = jnp.where(brand_new[None, :, :, None], fresh_values, value_block)
        query_rows = queries[owner_req]
        scores = jnp.einsum(
            "ckgd,kcjd->ckgj", query_rows, key_block, preferred_element_type=jnp.float32
        ) * head_dim ** (-0.5)
        shown = visible[:, None, None, :]
        scores = jnp.where(shown, scores, very_low)
        span_max = jnp.max(scores, axis=-1)
        weights = jnp.where(shown, jnp.exp(scores - span_max[..., None]), 0.0)
        span_total = jnp.sum(weights, axis=-1)
        span_sum = jnp.einsum(
            "ckgj,kcjd->ckgd",
            weights.astype(jnp.bfloat16),
            value_block,
            preferred_element_type=jnp.float32,
        )
        member = (block_req[None, :] == request_ids[:, None])[:, :, None, None]
        block_max = jnp.max(jnp.where(member, span_max[None], very_low), axis=1)
        new_max = jnp.maximum(top, block_max)
        factor = jnp.exp(jnp.where(member, span_max[None] - new_max[:, None], very_low))
        old_factor = jnp.exp(top - new_max)
        total = total * old_factor + jnp.sum(factor * span_total[None], axis=1)
        accum = accum * old_factor[..., None] + jnp.einsum("rckg,ckgd->rkgd", factor, span_sum)
        return (new_max, total, accum)

    starting = (
        jnp.full((requests, kv_local, group_size), very_low, jnp.float32),
        jnp.zeros((requests, kv_local, group_size), jnp.float32),
        jnp.zeros((requests, kv_local, group_size, head_dim), jnp.float32),
    )
    top, total, accum = lax.fori_loop(0, block_total, advance, starting)
    top, total, accum = joined((top, total, accum), ("grp", "mem"), blend)
    first_row = lax.axis_index("grp") * rows_grp
    total = lax.dynamic_slice_in_dim(total, first_row, rows_grp, 0)
    accum = lax.dynamic_slice_in_dim(accum, first_row, rows_grp, 0)
    attended = (
        (accum / total[..., None]).astype(jnp.bfloat16).reshape(rows_grp, heads_local * head_dim)
    )
    partial_out = jnp.dot(attended, w_out, preferred_element_type=jnp.float32)
    return lax.psum(partial_out, "tp").astype(jnp.bfloat16)


def solution(mesh):
    placed = (
        P("grp", "mem"),
        P("mem"),
        P("mem", "tp"),
        P(None, "mem", "tp"),
        P("tp", "mem"),
        P("tp", ("grp", "mem"), None, None),
        P("tp", ("grp", "mem"), None, None),
        P(),
        P(("grp", "mem")),
        P(("grp", "mem")),
        P(),
    )
    return jax.shard_map(
        per_device, mesh=mesh, in_specs=placed, out_specs=P("grp", "mem"), check_vma=False
    )
```

profile of v0, /device:TPU:2, one launch (start us, length us, event | category | flops | bytes accessed | tf_op | source)
XLA Modules:
  0.0 274.5 jit_solution(6258335628385906026)
XLA Ops:
  6.6 1.3 fusion.43
  8.0 1.2 fusion.45
  9.2 3.1 %fusion.56 = f32[16,1536]{1,0:T(8,128)S(1)} fusion(bf16[1536,1536]{1,0:T(8,128)(2,1)} %param.17, bf16[16,1536]{1,0:T(8,128)(2,1)} %param.15, f32[1536]{0:T(1024)} %param.16), kind=kOutput, calls=%fused_computation.87 | convolution fusion | flops 75571200 | bytes 4872192 | tf_op jit(solution)/shard_map/dot_general | solution.py:91
  13.2 14.9 %psum.22 = f32[16]{0:T(128)S(1)} all-reduce(f32[16]{0:T(128)S(1)} %fusion.50), channel_id=1, replica_groups=mesh['grp'=4,'tp'=8,'mem'=8] {'mem'}, use_global_device_ids=true, to_apply=%region_3.0 | all-reduce | flops 16 | bytes 128 | tf_op jit(solution)/shard_map/psum | solution.py:97
  29.6 49.1 %all-reduce.2.cloned.1.call-done = f32[16,1792]{1,0:T(8,128)} async-done(((f32[16,1792]{1,0:T(8,128)}), f32[16,1792]{1,0:T(8,128)}) %all-reduce.2.cloned.1.call-update) | async-done | bytes 114704 | tf_op jit(solution)/shard_map/psum | solution.py:97
  80.2 12.4 %all_gather.21 = bf16[64,1792]{1,0:T(8,128)(2,1)S(1)} all-gather(bf16[16,1792]{1,0:T(8,128)(2,1)S(1)} %pad_maximum_fusion.2), channel_id=1, replica_groups=mesh['grp'=4,'tp'=8,'mem'=8] {'grp'}, dimensions={0}, use_global_device_ids=true | all-gather | bytes 286720 | tf_op jit(solution)/shard_map/all_gather | solution.py:101
  92.9 12.3 %while.35 = (s32[]{:T(128)}, f32[64,1,12]{0,2,1:T(8,128)S(1)}, f32[64,1,12]{0,2,1:T(8,128)S(1)}, f32[64,1,12,128]{3,0,2,1:T(8,128)S(1)}, s32[]{:T(128)}, /*index...) while((s32[]{:T(128)}, f32[64,1,12]{0,2,1:T(8,128)S(1)}, ...), condition=%wide.region_9.10_spmd.clone, body=%wide.region_4.9_spmd.clone.sunk | while | flops 16785352 | bytes 2539323 | solution.py:162
  106.1 23.0 %all-gather = f32[2048,1,12]{2,1,0:T(1,128)S(1)} all-gather(f32[64,1,12]{2,1,0:T(1,128)S(1)} %copy.78), channel_id=2, replica_groups=mesh['grp'=4,'tp'=8,'mem'=8] {'grp','mem'}, dimensions={0}, use_global_device_ids=true | all-gather | bytes 101376 | tf_op jit(solution)/shard_map/all_gather | solution.py:15
  129.5 26.1 %all-gather.1 = f32[2048,1,12]{2,1,0:T(1,128)S(1)} all-gather(f32[64,1,12]{2,1,0:T(1,128)S(1)} %copy.79), channel_id=3, replica_groups=mesh['grp'=4,'tp'=8,'mem'=8] {'grp','mem'}, dimensions={0}, use_global_device_ids=true | all-gather | bytes 101376 | tf_op jit(solution)/shard_map/all_gather | solution.py:15
  156.1 19.0 %all-gather.5.cloned.1.call-done = f32[2048,1,12,128]{3,0,2,1:T(8,128)} async-done(((f32[64,1,12,128]{3,0,2,1:T(8,128)}), f32[2048,1,12,128]{3,0,2,1:T(8,128)}) %all-gather.5.cloned.1.call-update) | async-done | bytes 12582928 | tf_op jit(solution)/shard_map/all_gather | solution.py:15
  176.4 56.3 %while.34 = (s32[]{:T(128)}, f32[64,1,12]{0,1,2:T(1,128)S(1)}, f32[64,1,12]{0,1,2:T(1,128)S(1)}, f32[64,1,12,128]{3,2,1,0:T(8,128)S(1)}, f32[32,64,1,12]{1,2,3,0...) while((s32[]{:T(128)}, f32[64,1,12]{0,1,2:T(1,128)S(1)}, ...), condition=%wide.region_11.12_spmd, body=%wide.region_10.11_spmd.sunk | while | flops 299525 | bytes 2009239 | solution.py:21
  176.7 1.0 constant_dynamic-slice_fusion.2
  178.5 1.0 constant_dynamic-slice_fusion.2
  180.3 1.0 constant_dynamic-slice_fusion.2
  182.1 1.0 constant_dynamic-slice_fusion.2
  183.9 1.0 constant_dynamic-slice_fusion.2
  185.8 1.0 constant_dynamic-slice_fusion.2
  187.6 1.0 constant_dynamic-slice_fusion.2
  189.4 1.0 constant_dynamic-slice_fusion.2
  191.2 1.0 constant_dynamic-slice_fusion.2
  193.0 1.0 constant_dynamic-slice_fusion.2
  194.8 1.0 constant_dynamic-slice_fusion.2
  196.6 1.0 constant_dynamic-slice_fusion.2
  198.5 1.0 constant_dynamic-slice_fusion.2
  200.3 1.0 constant_dynamic-slice_fusion.2
  202.1 1.0 constant_dynamic-slice_fusion.2
  203.9 1.0 constant_dynamic-slice_fusion.2
  205.7 1.0 constant_dynamic-slice_fusion.2
  207.5 1.0 constant_dynamic-slice_fusion.2
  209.4 1.0 constant_dynamic-slice_fusion.2
  232.9 3.0 %fusion.51 = f32[16,1536]{1,0:T(8,128)S(1)} fusion(bf16[1536,1536]{1,0:T(8,128)(2,1)} %param.19, bf16[2,8,12,128]{3,2,1,0:T(8,128)(2,1)S(1)} %bitcast.116), kind=kOutput, calls=%fused_computation.83 | convolution fusion | flops 75497472 | bytes 4866048 | tf_op jit(solution)/shard_map/dot_general | solution.py:170
  236.0 31.7 %psum.23 = bf16[16,1536]{1,0:T(8,128)(2,1)} all-reduce(f32[16,1536]{1,0:T(8,128)S(1)} %fusion.51), channel_id=1, replica_groups=mesh['grp'=4,'tp'=8,'mem'=8] {'tp'}, use_global_device_ids=true, to_apply=%region_12.13 | all-reduce | flops 24576 | bytes 147456 | tf_op jit(solution)/shard_map/psum | solution.py:171
  (239 shorter events, 54.9 us)
Async XLA Ops:
  6.5 6.5 %copy-start.3 = (bf16[16,1536]{1,0:T(8,128)(2,1)S(1)}, bf16[16,1536]{1,0:T(8,128)(2,1)}, u32[]{:S(2)}) copy-start(bf16[16,1536]{1,0:T(8,128)(2,1)} %param.15) | copy-start | bytes 147460
  6.5 21.5 %copy-start = (s32[64]{0:T(128)S(1)}, s32[64]{0:T(128)}, u32[]{:S(2)}) copy-start(s32[64]{0:T(128)} %param.22) | copy-start | bytes 772
  6.5 21.7 %copy-start.4 = (s32[32]{0:T(128)S(1)}, s32[32]{0:T(128)}, u32[]{:S(2)}) copy-start(s32[32]{0:T(128)} %param.23) | copy-start | bytes 388
  6.5 86.3 %copy-start.5 = (bf16[1,32,128,128]{3,2,1,0:T(8,128)(2,1)S(1)}, bf16[1,32,128,128]{3,2,1,0:T(8,128)(2,1)}, u32[]{:S(2)}) copy-start(bf16[1,32,128,128]{3,2,1,0:T(8,128)(2,1)} %param.20) | copy-start | bytes 3145732
  6.5 86.3 %copy-start.6 = (bf16[1,32,128,128]{3,2,1,0:T(8,128)(2,1)S(1)}, bf16[1,32,128,128]{3,2,1,0:T(8,128)(2,1)}, u32[]{:S(2)}) copy-start(bf16[1,32,128,128]{3,2,1,0:T(8,128)(2,1)} %param.21) | copy-start | bytes 3145732
  6.5 86.3 %copy-start.7 = (s32[32]{0:T(128)S(1)}, s32[32]{0:T(128)}, u32[]{:S(2)}) copy-start(s32[32]{0:T(128)} %param.24) | copy-start | bytes 388
  6.6 86.3 %copy-start.1 = (s32[64]{0:T(128)S(1)}, s32[64]{0:T(128)}, u32[]{:S(2)}) copy-start(s32[64]{0:T(128)} %param.25) | copy-start | bytes 772
  6.6 72.1 %all-reduce.2.cloned.1.call-start = ((), (), s32[]{:S(2)}) async-start(), calls=%async_computation | async-start | bytes 229376 | tf_op jit(solution)/shard_map/psum | solution.py:97
  13.0 162.2 %all-gather.5.cloned.1.call-start = ((), (), s32[]{:S(2)}) async-start(), calls=%async_computation.1 | async-start | bytes 12976128 | tf_op jit(solution)/shard_map/all_gather | solution.py:15
  105.2 0.8 copy-start.2
Sparse Core Ops, SparseCore 0:
  13.1 65.5 all-reduce.1
  106.1 69.0 all-gather.4
where the time goes:
time: 276 us; the launch traced here: 274 us
  blocking collectives  108 us (39%)
  waiting for transfers between devices  68.2 us (25%)
  local copies, waits for them, and re-layouts  47.6 us (17%)
  other arithmetic  22.5 us (8%)
  between operations  14.3 us (5%)
  matrix products  12.8 us (5%)
    psum x1, waiting for transfers between devices, per_device(): summed, square_sum = lax.psum((projected, local_square), 'mem')  49.1 us
    all_gather x2, blocking collectives, joined(): everything = jax.tree.map(lambda part: lax.all_gather(part, axis), value)  49 us
    dynamic_slice x31, local copies, waits for them, and re-layouts, step(): return combine(so_far, jax.tree.map(lambda part: part[k], everything))  31.7 us
    psum x1, blocking collectives, per_device(): return lax.psum(partial_out, 'tp').astype(jnp.bfloat16)  31.7 us
    all_gather x1, waiting for transfers between devices, joined(): everything = jax.tree.map(lambda part: lax.all_gather(part, axis), value)  19 us
    add x31, other arithmetic, blend(): accum = first_part[2] * left[..., None] + second_part[2] * right[..., None]  16.6 us
    psum x1, blocking collectives, per_device(): summed, square_sum = lax.psum((projected, local_square), 'mem')  14.9 us
    all_gather x1, blocking collectives, per_device(): everything = lax.all_gather(own_rows, 'grp', axis=0, tiled=True)  12.4 us
  transfers between devices with their start and end apart: 2, of which 2 were waited for; matrix products, arithmetic and copies ran while one was open for 1% of the time, Pallas kernels for 0%

commit v1 on v0

v1 whole, which is shorter than its diff:
```python
import functools

import jax
import jax.numpy as jnp
from jax import lax
from jax.experimental import pallas as pl
from jax.experimental.pallas import tpu as pltpu
from jax.sharding import PartitionSpec as P

MESH = pl.DeviceIdType.MESH
HBM = pltpu.MemorySpace.HBM
D = 12288
epsilon = 1e-05
rope_base = 1000000.0
very_low = -1e30
SLOTS = 16
f32 = jnp.float32
bf16 = jnp.bfloat16


def chunks(count, width, body):
    def step(b, carry):
        stores = [body(b * width + u) for u in range(width)]
        for store in stores:
            store()
        return carry

    lax.fori_loop(0, count // width, step, 0)


def iota(shape, dim):
    return lax.broadcasted_iota(jnp.int32, shape, dim)


def kernel(
    n_grp, n_tp, n_mem,
    tokens, gain, w_query, w_keyval, w_out, key_cache, value_cache, req_len, span_request, span_first, new_slot,
    out,
    tok_v, gain_v, wq_v, wkv_v, wo_v, key_v, val_v, len_s, req_s, first_s, slot_s, lim_s, new_s, own_s,
    part, part_in, table, pick, col_req, leader, qkv, scores, maxima, tops, stat_top, spans,
    soft_out, soft_in, stat, blend, att, att_wide, sums, sums_in, done, local_sem, send_sem, recv_sem,
):
    g, t, m = lax.axis_index("grp"), lax.axis_index("tp"), lax.axis_index("mem")
    owners = n_grp * n_mem
    owner = g * n_mem + m
    rows, width = tok_v.shape
    requests = len_s.shape[0]
    own_rows = rows // n_mem
    out_rows = rows // n_tp
    spans_here = req_s.shape[0]
    q_cols = wq_v.shape[1]
    head_dim = key_v.shape[3]
    heads = q_cols // head_dim
    tile = own_rows * SLOTS
    k_chunks = 6
    k_step = width // k_chunks

    small = [
        pltpu.make_async_copy(req_len, len_s, local_sem.at[0]),
        pltpu.make_async_copy(span_request, req_s, local_sem.at[1]),
        pltpu.make_async_copy(span_first, first_s, local_sem.at[2]),
        pltpu.make_async_copy(new_slot, slot_s, local_sem.at[3]),
    ]
    tok_copy = pltpu.make_async_copy(tokens, tok_v, local_sem.at[4])
    gain_copy = pltpu.make_async_copy(gain, gain_v, local_sem.at[5])
    wkv_copy = pltpu.make_async_copy(w_keyval, wkv_v, local_sem.at[6])
    key_copy = pltpu.make_async_copy(key_cache, key_v, local_sem.at[7])
    val_copy = pltpu.make_async_copy(value_cache, val_v, local_sem.at[8])
    out_copy = pltpu.make_async_copy(w_out, wo_v, local_sem.at[9])
    wq_copies = [
        pltpu.make_async_copy(
            w_query.at[pl.ds(c * k_step, k_step), :], wq_v.at[pl.ds(c * k_step, k_step), :], local_sem.at[10 + c]
        )
        for c in range(k_chunks)
    ]
    tok_copy.start()
    gain_copy.start()
    for copy in wq_copies + [wkv_copy] + small + [key_copy, val_copy, out_copy]:
        copy.start()

    barrier = pltpu.get_barrier_semaphore()

    def owner_at(i):
        place = lax.rem(owner + i, owners)
        return place, {"grp": place // n_mem, "mem": lax.rem(place, n_mem)}

    def greet_owner(i, carry):
        pl.semaphore_signal(barrier, inc=1, device_id=owner_at(i)[1], device_id_type=MESH)
        return carry

    def greet_head(i, carry):
        pl.semaphore_signal(barrier, inc=1, device_id={"tp": lax.rem(t + i, n_tp)}, device_id_type=MESH)
        return carry

    lax.fori_loop(1, owners, greet_owner, 0)
    lax.fori_loop(1, n_tp, greet_head, 0)

    tok_copy.wait()
    gain_copy.wait()
    wide = tok_v[...].astype(f32)
    square = jnp.sum(wide * wide, axis=1, keepdims=True)
    scaled = (wide * gain_v[...].reshape(1, width)).astype(bf16)
    projected = jnp.zeros((rows, q_cols), f32)
    for c in range(k_chunks):
        wq_copies[c].wait()
        projected += jnp.dot(
            scaled[:, c * k_step : (c + 1) * k_step],
            wq_v[c * k_step : (c + 1) * k_step, :],
            preferred_element_type=f32,
        )
    wkv_copy.wait()
    new_part = [jnp.dot(scaled, wkv_v[i], preferred_element_type=f32) for i in range(2)]
    pieces = [projected[:, h * head_dim : (h + 1) * head_dim] for h in range(heads)] + new_part
    pieces += [jnp.broadcast_to(square, (rows, head_dim))]
    pieces += [jnp.zeros((rows, head_dim), f32)] * (SLOTS - len(pieces))
    for h, piece in enumerate(pieces):
        part[pl.ds(h, rows, stride=SLOTS), :] = piece

    pl.semaphore_wait(barrier, owners - 1 + n_tp - 1)

    def send_part(i, carry):
        to = lax.rem(m + i, n_mem)
        pltpu.make_async_remote_copy(
            src_ref=part.at[pl.ds(pl.multiple_of(to * tile, tile), tile), :],
            dst_ref=part_in.at[m],
            send_sem=send_sem.at[0],
            recv_sem=recv_sem.at[0],
            device_id={"mem": to},
            device_id_type=MESH,
        ).start()
        return carry

    lax.fori_loop(1, n_mem, send_part, 0)
    part_in[m] = part[pl.ds(pl.multiple_of(m * tile, tile), tile), :]

    for copy in small:
        copy.wait()
    lane = iota((1, head_dim), 1)
    own_len = [len_s[g * rows + m * own_rows + i] for i in range(own_rows)]
    position = jnp.where(iota((tile, 1), 0) < SLOTS, own_len[0], own_len[1]).astype(f32)
    half = head_dim // 2
    power = (lax.rem(lane, half).astype(f32) * 2.0) / head_dim
    frequency = jnp.exp(power * -jnp.log(jnp.full((1, head_dim), rope_base, f32)))
    angles = position * frequency
    slot_row = lax.rem(iota((tile, head_dim), 0), SLOTS)
    turned = slot_row < heads + 1
    cosine = jnp.where(turned, jnp.cos(angles), 1.0)
    sine = jnp.where(turned, jnp.sin(angles), 0.0)
    table[0] = cosine
    table[1] = jnp.where(lane < half, -sine, sine)

    def span_scalars(c, carry):
        r = jnp.maximum(req_s[c], 0)
        limit = jnp.where(req_s[c] >= 0, len_s[r] - first_s[c], -1)
        lim_s[c] = limit
        new_s[c] = jnp.where(slot_s[r] == owner * spans_here + c, limit, -1)
        own_s[c] = r
        return carry

    lax.fori_loop(0, spans_here, span_scalars, 0)

    flat = spans_here * SLOTS
    column = iota((1, flat), 1)
    target = jnp.zeros((1, flat), jnp.int32)
    in_rows = iota((spans_here, head_dim), 0)
    by_row = jnp.zeros((spans_here, head_dim), jnp.int32)
    for c in range(spans_here):
        target = jnp.where(column // SLOTS == c, req_s[c] * SLOTS, target)
        by_row = jnp.where(in_rows == c, req_s[c], by_row)
    target = target + lax.rem(column, SLOTS)
    col_req[...] = by_row
    first_of = jnp.ones((spans_here, head_dim), f32)
    for c in range(spans_here):
        first_of = jnp.where((by_row == req_s[c]) & (in_rows > c), 0.0, first_of)
    leader[...] = first_of

    pick_rows = 128

    def fill_pick(b, carry):
        at = pl.multiple_of(b * pick_rows, pick_rows)
        row = iota((pick_rows, flat), 0) + at
        pick[pl.ds(at, pick_rows), :] = jnp.where(row == target, 1.0, 0.0).astype(bf16)
        return carry

    lax.fori_loop(0, requests * SLOTS // pick_rows, fill_pick, 0)

    def wait_for(buffer, amount, kind):
        ref = buffer.at[pl.ds(0, amount)]
        pltpu.make_async_copy(ref, ref, kind).wait()

    wait_for(part_in, n_mem - 1, recv_sem.at[0])
    total = part_in[0]
    for i in range(1, n_mem):
        total = total + part_in[i]
    normed = []
    for i in range(own_rows):
        block = total[i * SLOTS : (i + 1) * SLOTS]
        root_mean = jnp.sqrt(block[heads + 2 : heads + 3] / D + epsilon)
        normed.append(block / root_mean)
    normed = jnp.concatenate(normed, axis=0)
    finished = normed * table[0] + pltpu.roll(normed, half, axis=1) * table[1]
    qkv[pl.ds(owner * own_rows, own_rows)] = finished.astype(bf16).reshape(own_rows, SLOTS, head_dim)

    def send_rows(i, carry):
        here = pl.ds(owner * own_rows, own_rows)
        pltpu.make_async_remote_copy(
            src_ref=qkv.at[here],
            dst_ref=qkv.at[here],
            send_sem=send_sem.at[1],
            recv_sem=recv_sem.at[1],
            device_id=owner_at(i)[1],
            device_id_type=MESH,
        ).start()
        return carry

    lax.fori_loop(1, owners, send_rows, 0)
    key_copy.wait()
    val_copy.wait()
    wait_for(qkv, (owners - 1) * own_rows, recv_sem.at[1])

    scale = head_dim**-0.5
    head = iota((SLOTS, head_dim), 0)
    lanes = iota((SLOTS, head_dim), 1)
    diagonal = lanes == head
    repeated = lax.rem(lanes, SLOTS) == head

    def score(c):
        tile_c = qkv[own_s[c]]
        raw = lax.dot_general(tile_c, key_v[0, c], (((1,), (1,)), ((), ())), preferred_element_type=f32)
        tile_wide = tile_c.astype(f32)
        fresh = jnp.sum(tile_wide * tile_wide[heads : heads + 1], axis=1, keepdims=True)
        shown = jnp.where(lanes <= lim_s[c], jnp.where(lanes == new_s[c], fresh, raw) * scale, very_low)
        top = jnp.max(shown, axis=1, keepdims=True)
        top_row = jnp.sum(jnp.where(repeated, top, 0.0), axis=0, keepdims=True)

        def store():
            scores[c] = shown
            maxima[pl.ds(c, 1), :] = top_row

        return store

    chunks(spans_here, 8, score)
    every = maxima[...]
    request_top = every
    for c in range(spans_here):
        request_top = jnp.maximum(request_top, jnp.where(col_req[...] == req_s[c], every[c : c + 1], very_low))
    tops[...] = request_top
    group = lane // SLOTS
    high = request_top.astype(bf16).astype(f32)
    middle = (request_top - high).astype(bf16).astype(f32)
    low = request_top - high - middle
    told = jnp.where(group == 2, high, jnp.where(group == 3, middle, jnp.where(group == 4, low, 0.0)))
    stat_top[...] = told * leader[...]

    def weigh(c):
        tile_c = qkv[own_s[c]]
        top = jnp.sum(jnp.where(diagonal, tops[pl.ds(c, 1), :], 0.0), axis=1, keepdims=True)
        weights = jnp.exp(scores[c] - top)
        total = jnp.sum(weights, axis=1, keepdims=True)
        is_new = lanes == new_s[c]
        fresh = jnp.sum(jnp.where(is_new, weights, 0.0), axis=1, keepdims=True)
        rounded = jnp.where(is_new, 0.0, weights).astype(bf16)
        value = jnp.dot(rounded, val_v[0, c], preferred_element_type=f32)
        value += fresh.astype(bf16).astype(f32) * tile_c[heads + 1 : heads + 2].astype(f32)
        total_row = jnp.sum(jnp.where(repeated, total, 0.0), axis=0, keepdims=True)
        total_high = total_row.astype(bf16).astype(f32)
        row = jnp.where(group == 0, total_high, jnp.where(group == 1, total_row - total_high, stat_top[pl.ds(c, 1), :]))
        result = jnp.where(head == heads, row, value).astype(bf16)

        def store():
            spans[pl.ds(pl.multiple_of(c * SLOTS, SLOTS), SLOTS), :] = result

        return store

    chunks(spans_here, 8, weigh)

    parts = 4
    at_once = owners // parts

    def gather(b, carry):
        at = pl.multiple_of(b * at_once * tile, at_once * tile)
        summed = jnp.dot(pick[pl.ds(at, at_once * tile), :], spans[...], preferred_element_type=f32)
        soft_out[pl.ds(b * at_once, at_once)] = summed.astype(bf16).reshape(at_once, tile, head_dim)
        return carry

    lax.fori_loop(0, parts, gather, 0)

    def send_soft(i, carry):
        place, device = owner_at(i)
        pltpu.make_async_remote_copy(
            src_ref=soft_out.at[place],
            dst_ref=soft_in.at[owner],
            send_sem=send_sem.at[2],
            recv_sem=recv_sem.at[2],
            device_id=device,
            device_id_type=MESH,
        ).start()
        return carry

    lax.fori_loop(1, owners, send_soft, 0)
    soft_in[owner] = soft_out[owner]
    wait_for(soft_in, owners - 1, recv_sem.at[2])

    def read_stat(s):
        lower = [soft_in[s, i * SLOTS : (i + 1) * SLOTS, :].astype(f32)[heads : heads + 1] for i in range(own_rows)]

        def store():
            for i in range(own_rows):
                stat[i, pl.ds(s, 1), :] = lower[i]

        return store

    chunks(owners, 8, read_stat)
    for i in range(own_rows):
        said = stat[i]

        def lanes_from(k):
            return pltpu.roll(said, head_dim - k * SLOTS, axis=1)

        total = said + lanes_from(1)
        top = jnp.where(total > 0.0, lanes_from(2) + lanes_from(3) + lanes_from(4), very_low)
        factor = jnp.exp(top - jnp.max(top, axis=0, keepdims=True))
        blend[i] = factor / jnp.sum(factor * total, axis=0, keepdims=True)

    def join(b, carry):
        sums_now = list(carry)
        for u in range(8):
            s = b * 8 + u
            for i in range(own_rows):
                factor = jnp.sum(jnp.where(diagonal, blend[i, pl.ds(s, 1), :], 0.0), axis=1, keepdims=True)
                sums_now[i] = sums_now[i] + factor * soft_in[s, i * SLOTS : (i + 1) * SLOTS, :].astype(f32)
        return tuple(sums_now)

    joined = lax.fori_loop(0, owners // 8, join, tuple(jnp.zeros((SLOTS, head_dim), f32) for _ in range(own_rows)))
    for i in range(own_rows):
        att[m * own_rows + i] = joined[i].astype(bf16)

    def send_att(i, carry):
        here = pl.ds(m * own_rows, own_rows)
        pltpu.make_async_remote_copy(
            src_ref=att.at[here],
            dst_ref=att.at[here],
            send_sem=send_sem.at[3],
            recv_sem=recv_sem.at[3],
            device_id={"mem": lax.rem(m + i, n_mem)},
            device_id_type=MESH,
        ).start()
        return carry

    lax.fori_loop(1, n_mem, send_att, 0)
    out_copy.wait()
    wait_for(att, (n_mem - 1) * own_rows, recv_sem.at[3])

    att_wide[...] = att[...].astype(f32).reshape(rows * SLOTS, head_dim)
    left = jnp.concatenate([att_wide[pl.ds(h, rows, stride=SLOTS), :] for h in range(heads)], axis=1).astype(bf16)
    product = jnp.dot(left, wo_v[...], preferred_element_type=f32)
    out_cols = product.shape[1] // head_dim
    for n in range(out_cols):
        sums[pl.ds(n, rows, stride=out_cols), :] = product[:, n * head_dim : (n + 1) * head_dim]

    slab = out_rows * out_cols

    def send_sums(i, carry):
        to = lax.rem(t + i, n_tp)
        pltpu.make_async_remote_copy(
            src_ref=sums.at[pl.ds(pl.multiple_of(to * slab, 8), slab), :],
            dst_ref=sums_in.at[t],
            send_sem=send_sem.at[4],
            recv_sem=recv_sem.at[4],
            device_id={"tp": to},
            device_id_type=MESH,
        ).start()
        return carry

    lax.fori_loop(1, n_tp, send_sums, 0)
    sums_in[t] = sums[pl.ds(pl.multiple_of(t * slab, 8), slab), :]
    wait_for(sums_in, n_tp - 1, recv_sem.at[4])
    total = sums_in[0]
    for i in range(1, n_tp):
        total = total + sums_in[i]
    here = pl.ds(pl.multiple_of(t * slab, 8), slab)
    done[here, :] = total

    def send_done(i, carry):
        pltpu.make_async_remote_copy(
            src_ref=done.at[here, :],
            dst_ref=done.at[here, :],
            send_sem=send_sem.at[5],
            recv_sem=recv_sem.at[5],
            device_id={"tp": lax.rem(t + i, n_tp)},
            device_id_type=MESH,
        ).start()
        return carry

    lax.fori_loop(1, n_tp, send_done, 0)
    wait_for(done, (n_tp - 1) * slab, recv_sem.at[5])
    for n in range(out_cols):
        out[:, n * head_dim : (n + 1) * head_dim] = done[pl.ds(n, rows, stride=out_cols), :].astype(bf16)

    wait_for(part, (n_mem - 1) * tile, send_sem.at[0])
    wait_for(qkv, (owners - 1) * own_rows, send_sem.at[1])
    wait_for(soft_out, owners - 1, send_sem.at[2])
    wait_for(att, (n_mem - 1) * own_rows, send_sem.at[3])
    wait_for(sums, (n_tp - 1) * slab, send_sem.at[4])
    wait_for(done, (n_tp - 1) * slab, send_sem.at[5])


def per_device(n_grp, n_tp, n_mem, *args):
    tokens, norm_gain, w_query, w_keyval, w_out, key_cache, value_cache, req_len, span_request, _, _ = args
    rows, width = tokens.shape
    q_cols = w_query.shape[1]
    head_dim = key_cache.shape[3]
    spans_here = span_request.shape[0]
    requests = req_len.shape[0]
    owners = n_grp * n_mem
    own_rows = rows // n_mem
    tile = own_rows * SLOTS
    out_width = w_out.shape[1]
    slab = rows // n_tp * out_width // head_dim
    scratch = [
        pltpu.VMEM(tokens.shape, bf16),
        pltpu.VMEM(norm_gain.shape, f32),
        pltpu.VMEM(w_query.shape, bf16),
        pltpu.VMEM(w_keyval.shape, bf16),
        pltpu.VMEM(w_out.shape, bf16),
        pltpu.VMEM(key_cache.shape, bf16),
        pltpu.VMEM(value_cache.shape, bf16),
        pltpu.SMEM((requests,), jnp.int32),
        pltpu.SMEM((spans_here,), jnp.int32),
        pltpu.SMEM((spans_here,), jnp.int32),
        pltpu.SMEM((requests,), jnp.int32),
        pltpu.SMEM((spans_here,), jnp.int32),
        pltpu.SMEM((spans_here,), jnp.int32),
        pltpu.SMEM((spans_here,), jnp.int32),
        pltpu.VMEM((rows * SLOTS, head_dim), f32),
        pltpu.VMEM((n_mem, tile, head_dim), f32),
        pltpu.VMEM((2, tile, head_dim), f32),
        pltpu.VMEM((requests * SLOTS, spans_here * SLOTS), bf16),
        pltpu.VMEM((spans_here, head_dim), jnp.int32),
        pltpu.VMEM((spans_here, head_dim), f32),
        pltpu.VMEM((requests, SLOTS, head_dim), bf16),
        pltpu.VMEM((spans_here, SLOTS, head_dim), f32),
        pltpu.VMEM((spans_here, head_dim), f32),
        pltpu.VMEM((spans_here, head_dim), f32),
        pltpu.VMEM((spans_here, head_dim), f32),
        pltpu.VMEM((spans_here * SLOTS, head_dim), bf16),
        pltpu.VMEM((owners, tile, head_dim), bf16),
        pltpu.VMEM((owners, tile, head_dim), bf16),
        pltpu.VMEM((own_rows, owners, head_dim), f32),
        pltpu.VMEM((own_rows, owners, head_dim), f32),
        pltpu.VMEM((rows, SLOTS, head_dim), bf16),
        pltpu.VMEM((rows * SLOTS, head_dim), f32),
        pltpu.VMEM((rows * out_width // head_dim, head_dim), f32),
        pltpu.VMEM((n_tp, slab, head_dim), f32),
        pltpu.VMEM((rows * out_width // head_dim, head_dim), f32),
        pltpu.SemaphoreType.DMA((16,)),
        pltpu.SemaphoreType.DMA((6,)),
        pltpu.SemaphoreType.DMA((6,)),
    ]
    return pl.pallas_call(
        functools.partial(kernel, n_grp, n_tp, n_mem),
        out_shape=jax.ShapeDtypeStruct((rows, out_width), bf16),
        in_specs=[pl.BlockSpec(memory_space=HBM)] * len(args),
        out_specs=pl.BlockSpec(memory_space=pltpu.VMEM),
        scratch_shapes=scratch,
        compiler_params=pltpu.CompilerParams(
            collective_id=0, has_side_effects=True, vmem_limit_bytes=40 * 1024 * 1024
        ),
        cost_estimate=pl.CostEstimate(flops=200_000_000, bytes_accessed=12_600_000, transcendentals=100_000),
    )(*args)


def solution(mesh):
    placed = (
        P("grp", "mem"),
        P("mem"),
        P("mem", "tp"),
        P(None, "mem", "tp"),
        P("tp", "mem"),
        P("tp", ("grp", "mem"), None, None),
        P("tp", ("grp", "mem"), None, None),
        P(),
        P(("grp", "mem")),
        P(("grp", "mem")),
        P(),
    )
    body = functools.partial(per_device, mesh.shape["grp"], mesh.shape["tp"], mesh.shape["mem"])
    return jax.shard_map(body, mesh=mesh, in_specs=placed, out_specs=P("grp", "mem"), check_vma=False)
```

time: 276 us -> 59.5 us (0.22)
  the two profiles are of different devices: /device:TPU:2 before, /device:TPU:1 now
where the time goes in v1:
time: 59.5 us; the launch traced here: 58.7 us
  Pallas kernels  45.7 us (77%)
  local copies, waits for them, and re-layouts  13 us (22%)
    pallas_call x1, Pallas kernels, per_device(): pl.pallas_call(functools.partial(kernel, n_grp, n_tp, n_mem), out_shape=j...  45.7 us
    unnamed x23, local copies, waits for them, and re-layouts  13 us

profile of v1, /device:TPU:1, one launch (start us, length us, event | category | flops | bytes accessed | tf_op | source)
XLA Modules:
  0.0 58.7 jit_solution(7547190679727380146)
XLA Ops:
  0.0 0.0 copy-start
  0.0 2.3 %copy-done = bf16[1536,1536]{1,0:T(8,128)(2,1)S(1)} copy-done((bf16[1536,1536]{1,0:T(8,128)(2,1)S(1)}, bf16[1536,1536]{1,0:T(8,128)(2,1)}, u32[]{:S(2)}) %copy-start) | copy-done | bytes 4718616
  2.3 0.0 copy-start.1
  2.3 2.3 %copy-done.1 = bf16[1536,1536]{1,0:T(8,128)(2,1)S(1)} copy-done((bf16[1536,1536]{1,0:T(8,128)(2,1)S(1)}, bf16[1536,1536]{1,0:T(8,128)(2,1)}, u32[]{:S(2)}) %copy-start.1) | copy-done | bytes 4718616
  4.7 0.0 copy-start.2
  4.7 1.2 %copy-done.2 = bf16[1,32,128,128]{3,2,1,0:T(8,128)(2,1)S(1)} copy-done((bf16[1,32,128,128]{3,2,1,0:T(8,128)(2,1)S(1)}, bf16[1,32,128,128]{3,2,1,0:T(8,128)(2,1)}, u32[]{:S(2)}) %copy-start.2) | copy-done | bytes 1048600
  5.9 0.0 copy-start.3
  5.9 1.2 %copy-done.3 = bf16[1,32,128,128]{3,2,1,0:T(8,128)(2,1)S(1)} copy-done((bf16[1,32,128,128]{3,2,1,0:T(8,128)(2,1)S(1)}, bf16[1,32,128,128]{3,2,1,0:T(8,128)(2,1)}, u32[]{:S(2)}) %copy-start.3) | copy-done | bytes 1048600
  7.1 0.0 copy-start.4
  7.1 1.1 %copy-done.4 = bf16[2,1536,128]{2,1,0:T(8,128)(2,1)S(1)} copy-done((bf16[2,1536,128]{2,1,0:T(8,128)(2,1)S(1)}, bf16[2,1536,128]{2,1,0:T(8,128)(2,1)}, u32[]{:S(2)}) %copy-start.4) | copy-done | bytes 786456
  8.3 0.0 copy-start.5
  8.3 0.8 %copy-done.5 = bf16[16,1536]{1,0:T(8,128)(2,1)S(1)} copy-done((bf16[16,1536]{1,0:T(8,128)(2,1)S(1)}, bf16[16,1536]{1,0:T(8,128)(2,1)}, u32[]{:S(2)}) %copy-start.5) | copy-done | bytes 49176
  9.1 0.0 copy-start.6
  9.1 0.7 %copy-done.6 = f32[1536]{0:T(1024)S(1)} copy-done((f32[1536]{0:T(1024)S(1)}, f32[1536]{0:T(1024)}, u32[]{:S(2)}) %copy-start.6) | copy-done | bytes 6168
  9.8 0.0 copy-start.7
  9.8 0.7 %copy-done.7 = s32[64]{0:T(128)S(1)} copy-done((s32[64]{0:T(128)S(1)}, s32[64]{0:T(128)}, u32[]{:S(2)}) %copy-start.7) | copy-done | bytes 280
  10.4 0.0 copy-start.8
  10.4 0.7 %copy-done.8 = s32[32]{0:T(128)S(1)} copy-done((s32[32]{0:T(128)S(1)}, s32[32]{0:T(128)}, u32[]{:S(2)}) %copy-start.8) | copy-done | bytes 152
  11.1 0.0 copy-start.9
  11.1 0.7 %copy-done.9 = s32[32]{0:T(128)S(1)} copy-done((s32[32]{0:T(128)S(1)}, s32[32]{0:T(128)}, u32[]{:S(2)}) %copy-start.9) | copy-done | bytes 152
  11.7 0.0 copy-start.10
  11.7 0.7 %copy-done.10 = s32[64]{0:T(128)S(1)} copy-done((s32[64]{0:T(128)S(1)}, s32[64]{0:T(128)}, u32[]{:S(2)}) %copy-start.10) | copy-done | bytes 280
  12.4 45.7 %shard_map.109 = bf16[16,1536]{1,0:T(8,128)(2,1)S(1)} custom-call(bf16[16,1536]{1,0:T(8,128)(2,1)S(1)} %copy-done.5, f32[1536]{0:T(1024)S(1)} %copy-done.6, bf16[1536,1536]{1,0:T(8,128)(2,1)S(1)} %copy-done, bf16[2,1536,128]{2,1,0:T(8,128)(2,1)S(1)} %copy-done.4, bf16[1536,1536]{1,0:T(8,128)(2,1)S(1)} %copy-done.1, bf16[1,32,128,128]{3,2,1,0:T(8,128)(2,1)S(1)} %copy-done.2, ...), custom_call_target="tpu_custom_call" | custom-call | flops 200000000 | bytes 12600000 | tf_op jit(solution)/shard_map/pallas_call | solution.py:460
  58.1 0.6 %copy.13 = bf16[16,1536]{1,0:T(8,128)(2,1)} copy(bf16[16,1536]{1,0:T(8,128)(2,1)S(1)} %shard_map.109) | data formatting | bytes 98304
Async XLA Ops:
  0.0 2.3 %copy-start = (bf16[1536,1536]{1,0:T(8,128)(2,1)S(1)}, bf16[1536,1536]{1,0:T(8,128)(2,1)}, u32[]{:S(2)}) copy-start(bf16[1536,1536]{1,0:T(8,128)(2,1)} %w_query.1) | copy-start | bytes 14155780
  2.3 2.3 %copy-start.1 = (bf16[1536,1536]{1,0:T(8,128)(2,1)S(1)}, bf16[1536,1536]{1,0:T(8,128)(2,1)}, u32[]{:S(2)}) copy-start(bf16[1536,1536]{1,0:T(8,128)(2,1)} %w_out.1) | copy-start | bytes 14155780
  4.7 1.2 %copy-start.2 = (bf16[1,32,128,128]{3,2,1,0:T(8,128)(2,1)S(1)}, bf16[1,32,128,128]{3,2,1,0:T(8,128)(2,1)}, u32[]{:S(2)}) copy-start(bf16[1,32,128,128]{3,2,1,0:T(8,128)(2,1)} %key_cache.1) | copy-start | bytes 3145732
  5.9 1.2 %copy-start.3 = (bf16[1,32,128,128]{3,2,1,0:T(8,128)(2,1)S(1)}, bf16[1,32,128,128]{3,2,1,0:T(8,128)(2,1)}, u32[]{:S(2)}) copy-start(bf16[1,32,128,128]{3,2,1,0:T(8,128)(2,1)} %value_cache.1) | copy-start | bytes 3145732
  7.1 1.1 %copy-start.4 = (bf16[2,1536,128]{2,1,0:T(8,128)(2,1)S(1)}, bf16[2,1536,128]{2,1,0:T(8,128)(2,1)}, u32[]{:S(2)}) copy-start(bf16[2,1536,128]{2,1,0:T(8,128)(2,1)} %w_keyval.1) | copy-start | bytes 2359300
  8.3 0.8 %copy-start.5 = (bf16[16,1536]{1,0:T(8,128)(2,1)S(1)}, bf16[16,1536]{1,0:T(8,128)(2,1)}, u32[]{:S(2)}) copy-start(bf16[16,1536]{1,0:T(8,128)(2,1)} %tokens.1) | copy-start | bytes 147460
  9.1 0.7 %copy-start.6 = (f32[1536]{0:T(1024)S(1)}, f32[1536]{0:T(1024)}, u32[]{:S(2)}) copy-start(f32[1536]{0:T(1024)} %gain.1) | copy-start | bytes 18436
  9.8 0.7 %copy-start.7 = (s32[64]{0:T(128)S(1)}, s32[64]{0:T(128)}, u32[]{:S(2)}) copy-start(s32[64]{0:T(128)} %req_len.1) | copy-start | bytes 772
  10.4 0.7 %copy-start.8 = (s32[32]{0:T(128)S(1)}, s32[32]{0:T(128)}, u32[]{:S(2)}) copy-start(s32[32]{0:T(128)} %span_request.1) | copy-start | bytes 388
  11.1 0.7 %copy-start.9 = (s32[32]{0:T(128)S(1)}, s32[32]{0:T(128)}, u32[]{:S(2)}) copy-start(s32[32]{0:T(128)} %span_first.1) | copy-start | bytes 388
  11.7 0.7 %copy-start.10 = (s32[64]{0:T(128)S(1)}, s32[64]{0:T(128)}, u32[]{:S(2)}) copy-start(s32[64]{0:T(128)} %new_slot.1) | copy-start | bytes 772

commit v2 on v1

--- a/solution.py
+++ b/solution.py
@@ -28,6 +28,15 @@
     lax.fori_loop(0, count // width, step, 0)
 
 
+def hops(d, size):
+    return min(d, size - d)
+
+
+def far_first(size, each):
+    chips = sorted(range(size), key=lambda d: -hops(d, size))
+    return [d * each + c for d in chips for c in range(each)]
+
+
 def iota(shape, dim):
     return lax.broadcasted_iota(jnp.int32, shape, dim)
 
@@ -38,7 +47,7 @@
     out,
     tok_v, gain_v, wq_v, wkv_v, wo_v, key_v, val_v, len_s, req_s, first_s, slot_s, lim_s, new_s, own_s,
     part, part_in, table, pick, col_req, leader, qkv, scores, maxima, tops, stat_top, spans,
-    soft_out, soft_in, stat, blend, att, att_wide, sums, sums_in, done, local_sem, send_sem, recv_sem,
+    soft_out, soft_in, stat, blend, att, att_wide, wide_rows, sums, sums_in, done, local_sem, send_sem, recv_sem,
 ):
     g, t, m = lax.axis_index("grp"), lax.axis_index("tp"), lax.axis_index("mem")
     owners = n_grp * n_mem
@@ -75,25 +84,29 @@
     ]
     tok_copy.start()
     gain_copy.start()
-    for copy in wq_copies + [wkv_copy] + small + [key_copy, val_copy, out_copy]:
+    for copy in wq_copies + [wkv_copy] + small:
         copy.start()
 
     barrier = pltpu.get_barrier_semaphore()
 
-    def owner_at(i):
-        place = lax.rem(owner + i, owners)
-        return place, {"grp": place // n_mem, "mem": lax.rem(place, n_mem)}
-
-    def greet_owner(i, carry):
-        pl.semaphore_signal(barrier, inc=1, device_id=owner_at(i)[1], device_id_type=MESH)
-        return carry
-
-    def greet_head(i, carry):
-        pl.semaphore_signal(barrier, inc=1, device_id={"tp": lax.rem(t + i, n_tp)}, device_id_type=MESH)
-        return carry
-
-    lax.fori_loop(1, owners, greet_owner, 0)
-    lax.fori_loop(1, n_tp, greet_head, 0)
+    def owner_at(dg, dm):
+        to_g = lax.rem(g + dg, n_grp)
+        to_m = lax.rem(m // 2 + dm // 2, n_mem // 2) * 2 + lax.rem(m + dm, 2)
+        return to_g * n_mem + to_m, {"grp": to_g, "mem": to_m}
+
+    mem_order = far_first(n_mem // 2, 2)
+    for dg in far_first(n_grp, 1):
+        for dm in mem_order:
+            if dg or dm:
+                pl.semaphore_signal(barrier, inc=1, device_id=owner_at(dg, dm)[1], device_id_type=MESH)
+    tp_order = [d for d in far_first(n_tp, 1) if d]
+    for d in tp_order:
+        pl.semaphore_signal(barrier, inc=1, device_id={"tp": lax.rem(t + d, n_tp)}, device_id_type=MESH)
+    mem_order = [d for d in mem_order if d]
+    owner_order = sorted(
+        [(dg, dm) for dg in range(n_grp) for dm in range(n_mem) if dg or dm],
+        key=lambda d: -hops(d[0], n_grp) - hops(d[1] // 2, n_mem // 2),
+    )
 
     tok_copy.wait()
     gain_copy.wait()
@@ -109,6 +122,8 @@
             preferred_element_type=f32,
         )
     wkv_copy.wait()
+    for copy in (key_copy, val_copy, out_copy):
+        copy.start()
     new_part = [jnp.dot(scaled, wkv_v[i], preferred_element_type=f32) for i in range(2)]
     pieces = [projected[:, h * head_dim : (h + 1) * head_dim] for h in range(heads)] + new_part
     pieces += [jnp.broadcast_to(square, (rows, head_dim))]
@@ -118,8 +133,8 @@
 
     pl.semaphore_wait(barrier, owners - 1 + n_tp - 1)
 
-    def send_part(i, carry):
-        to = lax.rem(m + i, n_mem)
+    for d in mem_order:
+        to = owner_at(0, d)[1]["mem"]
         pltpu.make_async_remote_copy(
             src_ref=part.at[pl.ds(pl.multiple_of(to * tile, tile), tile), :],
             dst_ref=part_in.at[m],
@@ -128,9 +143,6 @@
             device_id={"mem": to},
             device_id_type=MESH,
         ).start()
-        return carry
-
-    lax.fori_loop(1, n_mem, send_part, 0)
     part_in[m] = part[pl.ds(pl.multiple_of(m * tile, tile), tile), :]
 
     for copy in small:
@@ -201,19 +213,16 @@
     finished = normed * table[0] + pltpu.roll(normed, half, axis=1) * table[1]
     qkv[pl.ds(owner * own_rows, own_rows)] = finished.astype(bf16).reshape(own_rows, SLOTS, head_dim)
 
-    def send_rows(i, carry):
-        here = pl.ds(owner * own_rows, own_rows)
+    here = pl.ds(owner * own_rows, own_rows)
+    for d in owner_order:
         pltpu.make_async_remote_copy(
             src_ref=qkv.at[here],
             dst_ref=qkv.at[here],
             send_sem=send_sem.at[1],
             recv_sem=recv_sem.at[1],
-            device_id=owner_at(i)[1],
+            device_id=owner_at(*d)[1],
             device_id_type=MESH,
         ).start()
-        return carry
-
-    lax.fori_loop(1, owners, send_rows, 0)
     key_copy.wait()
     val_copy.wait()
     wait_for(qkv, (owners - 1) * own_rows, recv_sem.at[1])
@@ -274,30 +283,21 @@
 
     chunks(spans_here, 8, weigh)
 
-    parts = 4
-    at_once = owners // parts
-
-    def gather(b, carry):
-        at = pl.multiple_of(b * at_once * tile, at_once * tile)
-        summed = jnp.dot(pick[pl.ds(at, at_once * tile), :], spans[...], preferred_element_type=f32)
-        soft_out[pl.ds(b * at_once, at_once)] = summed.astype(bf16).reshape(at_once, tile, head_dim)
-        return carry
-
-    lax.fori_loop(0, parts, gather, 0)
-
-    def send_soft(i, carry):
-        place, device = owner_at(i)
-        pltpu.make_async_remote_copy(
-            src_ref=soft_out.at[place],
-            dst_ref=soft_in.at[owner],
-            send_sem=send_sem.at[2],
-            recv_sem=recv_sem.at[2],
-            device_id=device,
-            device_id_type=MESH,
-        ).start()
-        return carry
-
-    lax.fori_loop(1, owners, send_soft, 0)
+    for dg in far_first(n_grp, 1):
+        group_of = lax.rem(g + dg, n_grp)
+        at = pl.multiple_of(group_of * n_mem * tile, n_mem * tile)
+        summed = jnp.dot(pick[pl.ds(at, n_mem * tile), :], spans[...], preferred_element_type=f32)
+        soft_out[pl.ds(group_of * n_mem, n_mem)] = summed.astype(bf16).reshape(n_mem, tile, head_dim)
+        for d in mem_order if dg == 0 else mem_order + [0]:
+            place, device = owner_at(dg, d)
+            pltpu.make_async_remote_copy(
+                src_ref=soft_out.at[place],
+                dst_ref=soft_in.at[owner],
+                send_sem=send_sem.at[2],
+                recv_sem=recv_sem.at[2],
+                device_id=device,
+                device_id_type=MESH,
+            ).start()
     soft_in[owner] = soft_out[owner]
     wait_for(soft_in, owners - 1, recv_sem.at[2])
 
@@ -335,74 +335,66 @@
     for i in range(own_rows):
         att[m * own_rows + i] = joined[i].astype(bf16)
 
-    def send_att(i, carry):
-        here = pl.ds(m * own_rows, own_rows)
+    here = pl.ds(m * own_rows, own_rows)
+    for d in mem_order:
         pltpu.make_async_remote_copy(
             src_ref=att.at[here],
             dst_ref=att.at[here],
             send_sem=send_sem.at[3],
             recv_sem=recv_sem.at[3],
-            device_id={"mem": lax.rem(m + i, n_mem)},
+            device_id={"mem": owner_at(0, d)[1]["mem"]},
             device_id_type=MESH,
         ).start()
-        return carry
-
-    lax.fori_loop(1, n_mem, send_att, 0)
     out_copy.wait()
     wait_for(att, (n_mem - 1) * own_rows, recv_sem.at[3])
 
+    out_cols = wo_v.shape[1] // head_dim
+    slab = out_rows * SLOTS
+    for n in range(out_cols, SLOTS):
+        wide_rows[pl.ds(n, rows, stride=SLOTS), :] = jnp.zeros((rows, head_dim), f32)
     att_wide[...] = att[...].astype(f32).reshape(rows * SLOTS, head_dim)
     left = jnp.concatenate([att_wide[pl.ds(h, rows, stride=SLOTS), :] for h in range(heads)], axis=1).astype(bf16)
     product = jnp.dot(left, wo_v[...], preferred_element_type=f32)
-    out_cols = product.shape[1] // head_dim
     for n in range(out_cols):
-        sums[pl.ds(n, rows, stride=out_cols), :] = product[:, n * head_dim : (n + 1) * head_dim]
-
-    slab = out_rows * out_cols
-
-    def send_sums(i, carry):
-        to = lax.rem(t + i, n_tp)
+        wide_rows[pl.ds(n, rows, stride=SLOTS), :] = product[:, n * head_dim : (n + 1) * head_dim]
+    sums[...] = wide_rows[...].astype(bf16).reshape(n_tp, slab, head_dim)
+
+    for d in tp_order:
+        to = lax.rem(t + d, n_tp)
         pltpu.make_async_remote_copy(
-            src_ref=sums.at[pl.ds(pl.multiple_of(to * slab, 8), slab), :],
+            src_ref=sums.at[to],
             dst_ref=sums_in.at[t],
             send_sem=send_sem.at[4],
             recv_sem=recv_sem.at[4],
             device_id={"tp": to},
             device_id_type=MESH,
         ).start()
-        return carry
-
-    lax.fori_loop(1, n_tp, send_sums, 0)
-    sums_in[t] = sums[pl.ds(pl.multiple_of(t * slab, 8), slab), :]
+    sums_in[t] = sums[t]
     wait_for(sums_in, n_tp - 1, recv_sem.at[4])
-    total = sums_in[0]
+    total = sums_in[0].astype(f32)
     for i in range(1, n_tp):
-        total = total + sums_in[i]
-    here = pl.ds(pl.multiple_of(t * slab, 8), slab)
-    done[here, :] = total
-
-    def send_done(i, carry):
+        total = total + sums_in[i].astype(f32)
+    done[t] = total.astype(bf16)
+    for d in tp_order:
         pltpu.make_async_remote_copy(
-            src_ref=done.at[here, :],
-            dst_ref=done.at[here, :],
+            src_ref=done.at[t],
+            dst_ref=done.at[t],
             send_sem=send_sem.at[5],
             recv_sem=recv_sem.at[5],
-            device_id={"tp": lax.rem(t + i, n_tp)},
+            device_id={"tp": lax.rem(t + d, n_tp)},
             device_id_type=MESH,
         ).start()
-        return carry
-
-    lax.fori_loop(1, n_tp, send_done, 0)
-    wait_for(done, (n_tp - 1) * slab, recv_sem.at[5])
+    wait_for(done, n_tp - 1, recv_sem.at[5])
+    wide_rows[...] = done[...].astype(f32).reshape(rows * SLOTS, head_dim)
     for n in range(out_cols):
-        out[:, n * head_dim : (n + 1) * head_dim] = done[pl.ds(n, rows, stride=out_cols), :].astype(bf16)
+        out[:, n * head_dim : (n + 1) * head_dim] = wide_rows[pl.ds(n, rows, stride=SLOTS), :].astype(bf16)
 
     wait_for(part, (n_mem - 1) * tile, send_sem.at[0])
     wait_for(qkv, (owners - 1) * own_rows, send_sem.at[1])
     wait_for(soft_out, owners - 1, send_sem.at[2])
     wait_for(att, (n_mem - 1) * own_rows, send_sem.at[3])
-    wait_for(sums, (n_tp - 1) * slab, send_sem.at[4])
-    wait_for(done, (n_tp - 1) * slab, send_sem.at[5])
+    wait_for(sums, n_tp - 1, send_sem.at[4])
+    wait_for(done, n_tp - 1, send_sem.at[5])
 
 
 def per_device(n_grp, n_tp, n_mem, *args):
@@ -416,7 +408,7 @@
     own_rows = rows // n_mem
     tile = own_rows * SLOTS
     out_width = w_out.shape[1]
-    slab = rows // n_tp * out_width // head_dim
+    slab = rows // n_tp * SLOTS
     scratch = [
         pltpu.VMEM(tokens.shape, bf16),
         pltpu.VMEM(norm_gain.shape, f32),
@@ -450,9 +442,10 @@
         pltpu.VMEM((own_rows, owners, head_dim), f32),
         pltpu.VMEM((rows, SLOTS, head_dim), bf16),
         pltpu.VMEM((rows * SLOTS, head_dim), f32),
-        pltpu.VMEM((rows * out_width // head_dim, head_dim), f32),
-        pltpu.VMEM((n_tp, slab, head_dim), f32),
-        pltpu.VMEM((rows * out_width // head_dim, head_dim), f32),
+        pltpu.VMEM((rows * SLOTS, head_dim), f32),
+        pltpu.VMEM((n_tp, slab, head_dim), bf16),
+        pltpu.VMEM((n_tp, slab, head_dim), bf16),
+        pltpu.VMEM((n_tp, slab, head_dim), bf16),
         pltpu.SemaphoreType.DMA((16,)),
         pltpu.SemaphoreType.DMA((6,)),
         pltpu.SemaphoreType.DMA((6,)),
@@ -464,7 +457,7 @@
         out_specs=pl.BlockSpec(memory_space=pltpu.VMEM),
         scratch_shapes=scratch,
         compiler_params=pltpu.CompilerParams(
-            collective_id=0, has_side_effects=True, vmem_limit_bytes=40 * 1024 * 1024
+            collective_id=0, has_side_effects=True, vmem_limit_bytes=64 * 1024 * 1024
         ),
         cost_estimate=pl.CostEstimate(flops=200_000_000, bytes_accessed=12_600_000, transcendentals=100_000),
     )(*args)

time: 59.5 us -> 43.8 us (0.74); the launches traced: 58.7 us -> 43.7 us
  local copies, waits for them, and re-layouts: 13 us -> 1.42 us
  Pallas kernels: 45.7 us -> 42.2 us
    unnamed x23 -> x1, local copies, waits for them, and re-layouts: 13 us -> 1.42 us
    pallas_call x1, Pallas kernels: 45.7 us -> 42.2 us  [per_device(): pl.pallas_call(functools.partial(kernel, n_grp, n_tp, n_mem), out_shape=j...]
where the time goes in v2:
time: 43.8 us; the launch traced here: 43.7 us
  Pallas kernels  42.2 us (96%)
  local copies, waits for them, and re-layouts  1.42 us (3%)
    pallas_call x1, Pallas kernels, per_device(): pl.pallas_call(functools.partial(kernel, n_grp, n_tp, n_mem), out_shape=j...  42.2 us
    unnamed x1, local copies, waits for them, and re-layouts  1.42 us

profile of v2, /device:TPU:1, one launch (start us, length us, event | category | flops | bytes accessed | tf_op | source)
XLA Modules:
  0.0 43.7 jit_solution(4417453682724839298)
XLA Ops:
  0.0 42.2 %shard_map.109 = bf16[16,1536]{1,0:T(8,128)(2,1)} custom-call(bf16[16,1536]{1,0:T(8,128)(2,1)} %tokens.1, f32[1536]{0:T(1024)} %gain.1, bf16[1536,1536]{1,0:T(8,128)(2,1)} %w_query.1, bf16[2,1536,128]{2,1,0:T(8,128)(2,1)} %w_keyval.1, bf16[1536,1536]{1,0:T(8,128)(2,1)} %w_out.1, bf16[1,32,128,128]{3,2,1,0:T(8,128)(2,1)} %key_cache.1, ...), custom_call_target="tpu_custom_call" | custom-call | flops 200000000 | bytes 12600000 | tf_op jit(solution)/shard_map/pallas_call | solution.py:453
  42.2 1.4 %copy.13 = bf16[16,1536]{1,0:T(8,128)(2,1)} copy(bf16[16,1536]{1,0:T(8,128)(2,1)} %shard_map.109) | data formatting | bytes 98304

commit v3 on v2

--- a/solution.py
+++ b/solution.py
@@ -248,7 +248,7 @@
 
         return store
 
-    chunks(spans_here, 8, score)
+    chunks(spans_here, 32, score)
     every = maxima[...]
     request_top = every
     for c in range(spans_here):
@@ -281,7 +281,7 @@
 
         return store
 
-    chunks(spans_here, 8, weigh)
+    chunks(spans_here, 32, weigh)
 
     for dg in far_first(n_grp, 1):
         group_of = lax.rem(g + dg, n_grp)
@@ -452,15 +452,15 @@
     ]
     return pl.pallas_call(
         functools.partial(kernel, n_grp, n_tp, n_mem),
-        out_shape=jax.ShapeDtypeStruct((rows, out_width), bf16),
+        out_shape=pltpu.VMEM((rows, out_width), bf16),
         in_specs=[pl.BlockSpec(memory_space=HBM)] * len(args),
         out_specs=pl.BlockSpec(memory_space=pltpu.VMEM),
         scratch_shapes=scratch,
         compiler_params=pltpu.CompilerParams(
-            collective_id=0, has_side_effects=True, vmem_limit_bytes=64 * 1024 * 1024
+            collective_id=0, has_side_effects=True, vmem_limit_bytes=48 * 1024 * 1024
         ),
         cost_estimate=pl.CostEstimate(flops=200_000_000, bytes_accessed=12_600_000, transcendentals=100_000),
-    )(*args)
+    )(*[pltpu.with_memory_space_constraint(a, HBM) for a in args])
 
 
 def solution(mesh):

time: 43.8 us -> 41.1 us (0.938)
  Pallas kernels: 42.2 us -> 40.4 us
  local copies, waits for them, and re-layouts: 1.42 us -> 0.62 us
    pallas_call x1, Pallas kernels: 42.2 us -> 40.4 us  [per_device(): pl.pallas_call(functools.partial(kernel, n_grp, n_tp, n_mem), out_shape=p...]
    unnamed x1, local copies, waits for them, and re-layouts: 1.42 us -> 0.62 us
where the time goes in v3:
time: 41.1 us; the launch traced here: 41 us
  Pallas kernels  40.4 us (98%)
  local copies, waits for them, and re-layouts  0.62 us (2%)
    pallas_call x1, Pallas kernels, per_device(): pl.pallas_call(functools.partial(kernel, n_grp, n_tp, n_mem), out_shape=p...  40.4 us

profile of v3, /device:TPU:1, one launch (start us, length us, event | category | flops | bytes accessed | tf_op | source)
XLA Modules:
  0.0 41.0 jit_solution(2657767513668738436)
XLA Ops:
  0.0 40.4 %shard_map.109 = bf16[16,1536]{1,0:T(8,128)(2,1)S(1)} custom-call(bf16[16,1536]{1,0:T(8,128)(2,1)} %tokens.1, f32[1536]{0:T(1024)} %gain.1, bf16[1536,1536]{1,0:T(8,128)(2,1)} %w_query.1, bf16[2,1536,128]{2,1,0:T(8,128)(2,1)} %w_keyval.1, bf16[1536,1536]{1,0:T(8,128)(2,1)} %w_out.1, bf16[1,32,128,128]{3,2,1,0:T(8,128)(2,1)} %key_cache.1, ...), custom_call_target="tpu_custom_call" | custom-call | flops 200000000 | bytes 12600000 | tf_op jit(solution)/shard_map/pallas_call | solution.py:453
  40.4 0.6 %copy.13 = bf16[16,1536]{1,0:T(8,128)(2,1)} copy(bf16[16,1536]{1,0:T(8,128)(2,1)S(1)} %shard_map.109) | data formatting | bytes 98304

commit v4 on v3

--- a/solution.py
+++ b/solution.py
@@ -14,6 +14,7 @@
 rope_base = 1000000.0
 very_low = -1e30
 SLOTS = 16
+PAIR = 24
 f32 = jnp.float32
 bf16 = jnp.bfloat16
 
@@ -45,9 +46,9 @@
     n_grp, n_tp, n_mem,
     tokens, gain, w_query, w_keyval, w_out, key_cache, value_cache, req_len, span_request, span_first, new_slot,
     out,
-    tok_v, gain_v, wq_v, wkv_v, wo_v, key_v, val_v, len_s, req_s, first_s, slot_s, lim_s, new_s, own_s,
-    part, part_in, table, pick, col_req, leader, qkv, scores, maxima, tops, stat_top, spans,
-    soft_out, soft_in, stat, blend, att, att_wide, wide_rows, sums, sums_in, done, local_sem, send_sem, recv_sem,
+    tok_v, gain_v, wq_v, wkv_v, wo_v, key_v, val_v, len_s, req_s, first_s, lim_s, pair_s, odd_s,
+    part, part_in, table, pick, pick_stat, col_req, leader, qrows, newest, new_score, values, maxima, totals, factors, spans,
+    soft_out, soft_in, stat_out, stat_in, blend, att, att_wide, wide_rows, sums, sums_in, done, local_sem, send_sem, recv_sem,
 ):
     g, t, m = lax.axis_index("grp"), lax.axis_index("tp"), lax.axis_index("mem")
     owners = n_grp * n_mem
@@ -68,7 +69,6 @@
         pltpu.make_async_copy(req_len, len_s, local_sem.at[0]),
         pltpu.make_async_copy(span_request, req_s, local_sem.at[1]),
         pltpu.make_async_copy(span_first, first_s, local_sem.at[2]),
-        pltpu.make_async_copy(new_slot, slot_s, local_sem.at[3]),
     ]
     tok_copy = pltpu.make_async_copy(tokens, tok_v, local_sem.at[4])
     gain_copy = pltpu.make_async_copy(gain, gain_v, local_sem.at[5])
@@ -163,30 +163,36 @@
 
     def span_scalars(c, carry):
         r = jnp.maximum(req_s[c], 0)
-        limit = jnp.where(req_s[c] >= 0, len_s[r] - first_s[c], -1)
-        lim_s[c] = limit
-        new_s[c] = jnp.where(slot_s[r] == owner * spans_here + c, limit, -1)
-        own_s[c] = r
+        lim_s[c] = jnp.where(req_s[c] >= 0, len_s[r] - first_s[c], 0)
+        pair_s[c] = r // 2
+        odd_s[c] = lax.rem(r, 2)
         return carry
 
     lax.fori_loop(0, spans_here, span_scalars, 0)
 
     flat = spans_here * SLOTS
     column = iota((1, flat), 1)
-    target = jnp.zeros((1, flat), jnp.int32)
     in_rows = iota((spans_here, head_dim), 0)
+    by_column = jnp.zeros((1, flat), jnp.int32)
     by_row = jnp.zeros((spans_here, head_dim), jnp.int32)
+    stat_column = iota((1, 6 * spans_here), 1)
+    by_stat = jnp.zeros((1, 6 * spans_here), jnp.int32)
     for c in range(spans_here):
-        target = jnp.where(column // SLOTS == c, req_s[c] * SLOTS, target)
+        by_column = jnp.where(column // SLOTS == c, req_s[c], by_column)
         by_row = jnp.where(in_rows == c, req_s[c], by_row)
-    target = target + lax.rem(column, SLOTS)
+        by_stat = jnp.where(lax.rem(stat_column, spans_here) == c, req_s[c], by_stat)
     col_req[...] = by_row
     first_of = jnp.ones((spans_here, head_dim), f32)
     for c in range(spans_here):
         first_of = jnp.where((by_row == req_s[c]) & (in_rows > c), 0.0, first_of)
     leader[...] = first_of
-
-    pick_rows = 128
+    row_in = lax.rem(column, SLOTS)
+    nowhere = -requests * SLOTS
+    of_first = jnp.where(row_in < 12, row_in, nowhere)
+    of_second = jnp.where(row_in < 8, row_in + 16, jnp.where(row_in < 12, nowhere, row_in))
+    target = (by_column + 2) // 2 * PAIR - PAIR + jnp.where(lax.rem(by_column + 2, 2) == 1, of_second, of_first)
+    target = jnp.where(by_column < 0, nowhere, target)
+    pick_rows = 96
 
     def fill_pick(b, carry):
         at = pl.multiple_of(b * pick_rows, pick_rows)
@@ -194,7 +200,9 @@
         pick[pl.ds(at, pick_rows), :] = jnp.where(row == target, 1.0, 0.0).astype(bf16)
         return carry
 
-    lax.fori_loop(0, requests * SLOTS // pick_rows, fill_pick, 0)
+    lax.fori_loop(0, owners * PAIR // pick_rows, fill_pick, 0)
+    wanted = iota((owners, 6 * spans_here), 0) * 2 + stat_column // (3 * spans_here)
+    pick_stat[...] = jnp.where(wanted == by_stat, 1.0, 0.0).astype(bf16)
 
     def wait_for(buffer, amount, kind):
         ref = buffer.at[pl.ds(0, amount)]
@@ -211,70 +219,101 @@
         normed.append(block / root_mean)
     normed = jnp.concatenate(normed, axis=0)
     finished = normed * table[0] + pltpu.roll(normed, half, axis=1) * table[1]
-    qkv[pl.ds(owner * own_rows, own_rows)] = finished.astype(bf16).reshape(own_rows, SLOTS, head_dim)
-
-    here = pl.ds(owner * own_rows, own_rows)
+
+    def in_pair(block):
+        sub_row = iota((8, head_dim), 0)
+        middle = jnp.where(sub_row < 4, block[8:16], pltpu.roll(block[24:32], 4, axis=0))
+        return jnp.concatenate([block[0:8], middle, block[16:24]], axis=0)
+
+    qrows[owner] = in_pair(finished).astype(bf16)
+
     for d in owner_order:
         pltpu.make_async_remote_copy(
-            src_ref=qkv.at[here],
-            dst_ref=qkv.at[here],
+            src_ref=qrows.at[owner],
+            dst_ref=qrows.at[owner],
             send_sem=send_sem.at[1],
             recv_sem=recv_sem.at[1],
             device_id=owner_at(*d)[1],
             device_id_type=MESH,
         ).start()
+    scale = head_dim**-0.5
+    rounded = finished.astype(bf16).astype(f32)
+    pair_row = iota((PAIR, head_dim), 0)
+    pair_lane = iota((PAIR, head_dim), 1)
+    of_first = pair_row < 12
+    pair_diagonal = pair_lane == jnp.where(of_first, pair_row, jnp.where(pair_row < 16, pair_row + 32, pair_row + 16))
+    new_key = jnp.where(of_first, rounded[heads : heads + 1], rounded[SLOTS + heads : SLOTS + heads + 1])
+    newest[...] = jnp.where(of_first, rounded[heads + 1 : heads + 2], rounded[SLOTS + heads + 1 : SLOTS + heads + 2])
+    fresh = jnp.sum(in_pair(rounded) * new_key, axis=1, keepdims=True) * scale
+    new_score[...] = jnp.sum(jnp.where(pair_diagonal, fresh, 0.0), axis=0, keepdims=True)
     key_copy.wait()
     val_copy.wait()
-    wait_for(qkv, (owners - 1) * own_rows, recv_sem.at[1])
-
-    scale = head_dim**-0.5
+    wait_for(qrows, owners - 1, recv_sem.at[1])
+
     head = iota((SLOTS, head_dim), 0)
     lanes = iota((SLOTS, head_dim), 1)
     diagonal = lanes == head
     repeated = lax.rem(lanes, SLOTS) == head
 
-    def score(c):
-        tile_c = qkv[own_s[c]]
-        raw = lax.dot_general(tile_c, key_v[0, c], (((1,), (1,)), ((), ())), preferred_element_type=f32)
-        tile_wide = tile_c.astype(f32)
-        fresh = jnp.sum(tile_wide * tile_wide[heads : heads + 1], axis=1, keepdims=True)
-        shown = jnp.where(lanes <= lim_s[c], jnp.where(lanes == new_s[c], fresh, raw) * scale, very_low)
+    def query_of(c):
+        pair = qrows[pair_s[c]].astype(f32)
+        rows_of = [jnp.where(odd_s[c] == 1, pair[16:24], pair[0:8]), pair[8:16]]
+        return jnp.concatenate(rows_of, axis=0).astype(bf16)
+
+    def soften(c, raw):
+        shown = jnp.where(lanes < lim_s[c], raw * scale, very_low)
         top = jnp.max(shown, axis=1, keepdims=True)
+        weights = jnp.exp(shown - top)
+        total = jnp.sum(weights, axis=1, keepdims=True)
         top_row = jnp.sum(jnp.where(repeated, top, 0.0), axis=0, keepdims=True)
-
-        def store():
-            scores[c] = shown
-            maxima[pl.ds(c, 1), :] = top_row
-
-        return store
-
-    chunks(spans_here, 32, score)
+        total_row = jnp.sum(jnp.where(repeated, total, 0.0), axis=0, keepdims=True)
+        return weights.astype(bf16), top_row, total_row
+
+    all_spans = range(spans_here)
+    raws = [
+        lax.dot_general(query_of(c), key_v[0, c], (((1,), (1,)), ((), ())), preferred_element_type=f32)
+        for c in all_spans
+    ]
+    softened = [soften(c, raws[c]) for c in all_spans]
+    for c in all_spans:
+        values[c] = jnp.dot(softened[c][0], val_v[0, c], preferred_element_type=f32)
+    for c in all_spans:
+        maxima[c : c + 1, :] = softened[c][1]
+        totals[c : c + 1, :] = softened[c][2]
     every = maxima[...]
     request_top = every
     for c in range(spans_here):
         request_top = jnp.maximum(request_top, jnp.where(col_req[...] == req_s[c], every[c : c + 1], very_low))
-    tops[...] = request_top
+    factor = jnp.exp(every - request_top)
+    factors[...] = factor
     group = lane // SLOTS
-    high = request_top.astype(bf16).astype(f32)
-    middle = (request_top - high).astype(bf16).astype(f32)
-    low = request_top - high - middle
-    told = jnp.where(group == 2, high, jnp.where(group == 3, middle, jnp.where(group == 4, low, 0.0)))
-    stat_top[...] = told * leader[...]
+    said = jnp.where(lax.rem(group, 2) == 0, request_top * leader[...], factor * totals[...])
+    high = said.astype(bf16)
+    rest = said - high.astype(f32)
+    middle = rest.astype(bf16)
+    low = (rest - middle.astype(f32)).astype(bf16)
+    thirds = jnp.concatenate([high, middle, low], axis=0).astype(f32)
+    first_lanes = jnp.where(group < 2, thirds, 0.0).astype(bf16)
+    second_lanes = jnp.where((group == 2) | (group == 3), thirds, 0.0).astype(bf16)
+    stats = jnp.dot(
+        pick_stat[...], jnp.concatenate([first_lanes, second_lanes], axis=0), preferred_element_type=f32
+    )
+    stat_out[...] = stats.reshape(owners, 1, head_dim)
+    for d in owner_order:
+        place, device = owner_at(*d)
+        pltpu.make_async_remote_copy(
+            src_ref=stat_out.at[place],
+            dst_ref=stat_in.at[owner],
+            send_sem=send_sem.at[6],
+            recv_sem=recv_sem.at[6],
+            device_id=device,
+            device_id_type=MESH,
+        ).start()
+    stat_in[owner] = stat_out[owner]
 
     def weigh(c):
-        tile_c = qkv[own_s[c]]
-        top = jnp.sum(jnp.where(diagonal, tops[pl.ds(c, 1), :], 0.0), axis=1, keepdims=True)
-        weights = jnp.exp(scores[c] - top)
-        total = jnp.sum(weights, axis=1, keepdims=True)
-        is_new = lanes == new_s[c]
-        fresh = jnp.sum(jnp.where(is_new, weights, 0.0), axis=1, keepdims=True)
-        rounded = jnp.where(is_new, 0.0, weights).astype(bf16)
-        value = jnp.dot(rounded, val_v[0, c], preferred_element_type=f32)
-        value += fresh.astype(bf16).astype(f32) * tile_c[heads + 1 : heads + 2].astype(f32)
-        total_row = jnp.sum(jnp.where(repeated, total, 0.0), axis=0, keepdims=True)
-        total_high = total_row.astype(bf16).astype(f32)
-        row = jnp.where(group == 0, total_high, jnp.where(group == 1, total_row - total_high, stat_top[pl.ds(c, 1), :]))
-        result = jnp.where(head == heads, row, value).astype(bf16)
+        factor = jnp.sum(jnp.where(diagonal, factors[pl.ds(c, 1), :], 0.0), axis=1, keepdims=True)
+        result = (values[c] * factor).astype(bf16)
 
         def store():
             spans[pl.ds(pl.multiple_of(c * SLOTS, SLOTS), SLOTS), :] = result
@@ -285,9 +324,9 @@
 
     for dg in far_first(n_grp, 1):
         group_of = lax.rem(g + dg, n_grp)
-        at = pl.multiple_of(group_of * n_mem * tile, n_mem * tile)
-        summed = jnp.dot(pick[pl.ds(at, n_mem * tile), :], spans[...], preferred_element_type=f32)
-        soft_out[pl.ds(group_of * n_mem, n_mem)] = summed.astype(bf16).reshape(n_mem, tile, head_dim)
+        at = pl.multiple_of(group_of * n_mem * PAIR, n_mem * PAIR)
+        summed = jnp.dot(pick[pl.ds(at, n_mem * PAIR), :], spans[...], preferred_element_type=f32)
+        soft_out[pl.ds(group_of * n_mem, n_mem)] = summed.astype(bf16).reshape(n_mem, PAIR, head_dim)
         for d in mem_order if dg == 0 else mem_order + [0]:
             place, device = owner_at(dg, d)
             pltpu.make_async_remote_copy(
@@ -299,65 +338,54 @@
                 device_id_type=MESH,
             ).start()
     soft_in[owner] = soft_out[owner]
+    wait_for(stat_in, owners - 1, recv_sem.at[6])
+    stats = stat_in[...].reshape(owners, head_dim)
+    total = pltpu.roll(stats, head_dim - SLOTS, axis=1)
+    top = jnp.where(total > 0.0, stats, very_low)
+    new_top = new_score[...]
+    most = jnp.maximum(jnp.max(top, axis=0, keepdims=True), new_top)
+    factor = jnp.exp(top - most)
+    new_factor = jnp.exp(new_top - most)
+    whole = jnp.sum(factor * total, axis=0, keepdims=True) + new_factor
+    blend[...] = factor / whole
+    new_share = jnp.sum(jnp.where(pair_diagonal, new_factor / whole, 0.0), axis=1, keepdims=True)
     wait_for(soft_in, owners - 1, recv_sem.at[2])
 
-    def read_stat(s):
-        lower = [soft_in[s, i * SLOTS : (i + 1) * SLOTS, :].astype(f32)[heads : heads + 1] for i in range(own_rows)]
-
-        def store():
-            for i in range(own_rows):
-                stat[i, pl.ds(s, 1), :] = lower[i]
-
-        return store
-
-    chunks(owners, 8, read_stat)
-    for i in range(own_rows):
-        said = stat[i]
-
-        def lanes_from(k):
-            return pltpu.roll(said, head_dim - k * SLOTS, axis=1)
-
-        total = said + lanes_from(1)
-        top = jnp.where(total > 0.0, lanes_from(2) + lanes_from(3) + lanes_from(4), very_low)
-        factor = jnp.exp(top - jnp.max(top, axis=0, keepdims=True))
-        blend[i] = factor / jnp.sum(factor * total, axis=0, keepdims=True)
-
     def join(b, carry):
-        sums_now = list(carry)
-        for u in range(8):
-            s = b * 8 + u
-            for i in range(own_rows):
-                factor = jnp.sum(jnp.where(diagonal, blend[i, pl.ds(s, 1), :], 0.0), axis=1, keepdims=True)
-                sums_now[i] = sums_now[i] + factor * soft_in[s, i * SLOTS : (i + 1) * SLOTS, :].astype(f32)
-        return tuple(sums_now)
-
-    joined = lax.fori_loop(0, owners // 8, join, tuple(jnp.zeros((SLOTS, head_dim), f32) for _ in range(own_rows)))
-    for i in range(own_rows):
-        att[m * own_rows + i] = joined[i].astype(bf16)
-
-    here = pl.ds(m * own_rows, own_rows)
+        for u in range(16):
+            s = b * 16 + u
+            share = jnp.sum(jnp.where(pair_diagonal, blend[pl.ds(s, 1), :], 0.0), axis=1, keepdims=True)
+            carry = carry + share * soft_in[s].astype(f32)
+        return carry
+
+    att[m] = lax.fori_loop(0, owners // 16, join, new_share * newest[...]).astype(bf16)
+
     for d in mem_order:
         pltpu.make_async_remote_copy(
-            src_ref=att.at[here],
-            dst_ref=att.at[here],
+            src_ref=att.at[m],
+            dst_ref=att.at[m],
             send_sem=send_sem.at[3],
             recv_sem=recv_sem.at[3],
             device_id={"mem": owner_at(0, d)[1]["mem"]},
             device_id_type=MESH,
         ).start()
     out_copy.wait()
-    wait_for(att, (n_mem - 1) * own_rows, recv_sem.at[3])
+    wait_for(att, n_mem - 1, recv_sem.at[3])
 
     out_cols = wo_v.shape[1] // head_dim
-    slab = out_rows * SLOTS
-    for n in range(out_cols, SLOTS):
-        wide_rows[pl.ds(n, rows, stride=SLOTS), :] = jnp.zeros((rows, head_dim), f32)
-    att_wide[...] = att[...].astype(f32).reshape(rows * SLOTS, head_dim)
-    left = jnp.concatenate([att_wide[pl.ds(h, rows, stride=SLOTS), :] for h in range(heads)], axis=1).astype(bf16)
+    att_wide[...] = att[...].astype(f32).reshape(n_mem * PAIR, head_dim)
+
+    def head_rows(h):
+        second = h + 16 if h < 8 else h + 4
+        return jnp.concatenate([att_wide[pl.ds(row, n_mem, stride=PAIR), :] for row in (h, second)], axis=0)
+
+    left = jnp.concatenate([head_rows(h) for h in range(heads)], axis=1).astype(bf16)
     product = jnp.dot(left, wo_v[...], preferred_element_type=f32)
     for n in range(out_cols):
-        wide_rows[pl.ds(n, rows, stride=SLOTS), :] = product[:, n * head_dim : (n + 1) * head_dim]
-    sums[...] = wide_rows[...].astype(bf16).reshape(n_tp, slab, head_dim)
+        for i in range(own_rows):
+            piece = product[i * n_mem : (i + 1) * n_mem, n * head_dim : (n + 1) * head_dim]
+            wide_rows[pl.ds(i * out_cols + n, n_mem, stride=own_rows * out_cols), :] = piece
+    sums[...] = wide_rows[...].astype(bf16).reshape(n_tp, out_rows * out_cols, head_dim)
 
     for d in tp_order:
         to = lax.rem(t + d, n_tp)
@@ -385,14 +413,15 @@
             device_id_type=MESH,
         ).start()
     wait_for(done, n_tp - 1, recv_sem.at[5])
-    wide_rows[...] = done[...].astype(f32).reshape(rows * SLOTS, head_dim)
+    wide_rows[...] = done[...].astype(f32).reshape(rows * out_cols, head_dim)
     for n in range(out_cols):
-        out[:, n * head_dim : (n + 1) * head_dim] = wide_rows[pl.ds(n, rows, stride=SLOTS), :].astype(bf16)
+        out[:, n * head_dim : (n + 1) * head_dim] = wide_rows[pl.ds(n, rows, stride=out_cols), :].astype(bf16)
 
     wait_for(part, (n_mem - 1) * tile, send_sem.at[0])
-    wait_for(qkv, (owners - 1) * own_rows, send_sem.at[1])
+    wait_for(qrows, owners - 1, send_sem.at[1])
     wait_for(soft_out, owners - 1, send_sem.at[2])
-    wait_for(att, (n_mem - 1) * own_rows, send_sem.at[3])
+    wait_for(stat_out, owners - 1, send_sem.at[6])
+    wait_for(att, n_mem - 1, send_sem.at[3])
     wait_for(sums, n_tp - 1, send_sem.at[4])
     wait_for(done, n_tp - 1, send_sem.at[5])
 
@@ -408,7 +437,7 @@
     own_rows = rows // n_mem
     tile = own_rows * SLOTS
     out_width = w_out.shape[1]
-    slab = rows // n_tp * SLOTS
+    slab = rows // n_tp * out_width // head_dim
     scratch = [
         pltpu.VMEM(tokens.shape, bf16),
         pltpu.VMEM(norm_gain.shape, f32),
@@ -420,35 +449,38 @@
         pltpu.SMEM((requests,), jnp.int32),
         pltpu.SMEM((spans_here,), jnp.int32),
         pltpu.SMEM((spans_here,), jnp.int32),
-        pltpu.SMEM((requests,), jnp.int32),
         pltpu.SMEM((spans_here,), jnp.int32),
         pltpu.SMEM((spans_here,), jnp.int32),
         pltpu.SMEM((spans_here,), jnp.int32),
         pltpu.VMEM((rows * SLOTS, head_dim), f32),
         pltpu.VMEM((n_mem, tile, head_dim), f32),
         pltpu.VMEM((2, tile, head_dim), f32),
-        pltpu.VMEM((requests * SLOTS, spans_here * SLOTS), bf16),
+        pltpu.VMEM((owners * PAIR, spans_here * SLOTS), bf16),
+        pltpu.VMEM((owners, 6 * spans_here), bf16),
         pltpu.VMEM((spans_here, head_dim), jnp.int32),
         pltpu.VMEM((spans_here, head_dim), f32),
-        pltpu.VMEM((requests, SLOTS, head_dim), bf16),
+        pltpu.VMEM((owners, PAIR, head_dim), bf16),
+        pltpu.VMEM((PAIR, head_dim), f32),
+        pltpu.VMEM((1, head_dim), f32),
         pltpu.VMEM((spans_here, SLOTS, head_dim), f32),
         pltpu.VMEM((spans_here, head_dim), f32),
         pltpu.VMEM((spans_here, head_dim), f32),
         pltpu.VMEM((spans_here, head_dim), f32),
         pltpu.VMEM((spans_here * SLOTS, head_dim), bf16),
-        pltpu.VMEM((owners, tile, head_dim), bf16),
-        pltpu.VMEM((owners, tile, head_dim), bf16),
-        pltpu.VMEM((own_rows, owners, head_dim), f32),
-        pltpu.VMEM((own_rows, owners, head_dim), f32),
-        pltpu.VMEM((rows, SLOTS, head_dim), bf16),
-        pltpu.VMEM((rows * SLOTS, head_dim), f32),
-        pltpu.VMEM((rows * SLOTS, head_dim), f32),
+        pltpu.VMEM((owners, PAIR, head_dim), bf16),
+        pltpu.VMEM((owners, PAIR, head_dim), bf16),
+        pltpu.VMEM((owners, 1, head_dim), f32),
+        pltpu.VMEM((owners, 1, head_dim), f32),
+        pltpu.VMEM((owners, head_dim), f32),
+        pltpu.VMEM((n_mem, PAIR, head_dim), bf16),
+        pltpu.VMEM((n_mem * PAIR, head_dim), f32),
+        pltpu.VMEM((n_tp * slab, head_dim), f32),
         pltpu.VMEM((n_tp, slab, head_dim), bf16),
         pltpu.VMEM((n_tp, slab, head_dim), bf16),
         pltpu.VMEM((n_tp, slab, head_dim), bf16),
         pltpu.SemaphoreType.DMA((16,)),
-        pltpu.SemaphoreType.DMA((6,)),
-        pltpu.SemaphoreType.DMA((6,)),
+        pltpu.SemaphoreType.DMA((7,)),
+        pltpu.SemaphoreType.DMA((7,)),
     ]
     return pl.pallas_call(
         functools.partial(kernel, n_grp, n_tp, n_mem),

time: 41.1 us -> 39.4 us (0.959)
  Pallas kernels: 40.4 us -> 38.6 us
    pallas_call x1, Pallas kernels: 40.4 us -> 38.6 us  [per_device(): pl.pallas_call(functools.partial(kernel, n_grp, n_tp, n_mem), out_shape=p...]
where the time goes in v4:
time: 39.4 us; the launch traced here: 39.3 us
  Pallas kernels  38.6 us (98%)
  local copies, waits for them, and re-layouts  0.62 us (2%)
    pallas_call x1, Pallas kernels, per_device(): pl.pallas_call(functools.partial(kernel, n_grp, n_tp, n_mem), out_shape=p...  38.6 us

profile of v4, /device:TPU:1, one launch (start us, length us, event | category | flops | bytes accessed | tf_op | source)
XLA Modules:
  0.0 39.3 jit_solution(4840732894093340068)
XLA Ops:
  0.0 38.6 %shard_map.109 = bf16[16,1536]{1,0:T(8,128)(2,1)S(1)} custom-call(bf16[16,1536]{1,0:T(8,128)(2,1)} %tokens.1, f32[1536]{0:T(1024)} %gain.1, bf16[1536,1536]{1,0:T(8,128)(2,1)} %w_query.1, bf16[2,1536,128]{2,1,0:T(8,128)(2,1)} %w_keyval.1, bf16[1536,1536]{1,0:T(8,128)(2,1)} %w_out.1, bf16[1,32,128,128]{3,2,1,0:T(8,128)(2,1)} %key_cache.1, ...), custom_call_target="tpu_custom_call" | custom-call | flops 200000000 | bytes 12600000 | tf_op jit(solution)/shard_map/pallas_call | solution.py:485
  38.6 0.6 %copy.13 = bf16[16,1536]{1,0:T(8,128)(2,1)} copy(bf16[16,1536]{1,0:T(8,128)(2,1)S(1)} %shard_map.109) | data formatting | bytes 98304

commit v5 on v4

--- a/solution.py
+++ b/solution.py
@@ -48,7 +48,7 @@
     out,
     tok_v, gain_v, wq_v, wkv_v, wo_v, key_v, val_v, len_s, req_s, first_s, lim_s, pair_s, odd_s,
     part, part_in, table, pick, pick_stat, col_req, leader, qrows, newest, new_score, values, maxima, totals, factors, spans,
-    soft_out, soft_in, stat_out, stat_in, blend, att, att_wide, wide_rows, sums, sums_in, done, local_sem, send_sem, recv_sem,
+    soft_out, soft_in, stat_out, stat_in, blend, att, att_wide, wide_rows, sums, sums_in, done, local_sem, send_sem, recv_sem, tp_sem,
 ):
     g, t, m = lax.axis_index("grp"), lax.axis_index("tp"), lax.axis_index("mem")
     owners = n_grp * n_mem
@@ -94,15 +94,20 @@
         to_m = lax.rem(m // 2 + dm // 2, n_mem // 2) * 2 + lax.rem(m + dm, 2)
         return to_g * n_mem + to_m, {"grp": to_g, "mem": to_m}
 
-    mem_order = far_first(n_mem // 2, 2)
-    for dg in far_first(n_grp, 1):
-        for dm in mem_order:
-            if dg or dm:
-                pl.semaphore_signal(barrier, inc=1, device_id=owner_at(dg, dm)[1], device_id_type=MESH)
+    mem_order = [d for d in far_first(n_mem // 2, 2) if d]
+    grp_order = [d for d in far_first(n_grp, 1) if d]
     tp_order = [d for d in far_first(n_tp, 1) if d]
-    for d in tp_order:
-        pl.semaphore_signal(barrier, inc=1, device_id={"tp": lax.rem(t + d, n_tp)}, device_id_type=MESH)
-    mem_order = [d for d in mem_order if d]
+    beside = (1, n_tp - 1)
+    for d in mem_order:
+        pl.semaphore_signal(barrier, inc=1, device_id=owner_at(0, d)[1], device_id_type=MESH)
+    for d in grp_order:
+        pl.semaphore_signal(barrier, inc=1, device_id=owner_at(d, 0)[1], device_id_type=MESH)
+
+    def tell_tp(semaphore, distances):
+        for d in distances:
+            pl.semaphore_signal(semaphore, inc=1, device_id={"tp": lax.rem(t + d, n_tp)}, device_id_type=MESH)
+
+    tell_tp(barrier, beside)
     owner_order = sorted(
         [(dg, dm) for dg in range(n_grp) for dm in range(n_mem) if dg or dm],
         key=lambda d: -hops(d[0], n_grp) - hops(d[1] // 2, n_mem // 2),
@@ -131,7 +136,8 @@
     for h, piece in enumerate(pieces):
         part[pl.ds(h, rows, stride=SLOTS), :] = piece
 
-    pl.semaphore_wait(barrier, owners - 1 + n_tp - 1)
+    pl.semaphore_wait(barrier, len(mem_order) + len(grp_order) + len(beside))
+    tell_tp(tp_sem.at[0], beside)
 
     for d in mem_order:
         to = owner_at(0, d)[1]["mem"]
@@ -236,6 +242,8 @@
             device_id=owner_at(*d)[1],
             device_id_type=MESH,
         ).start()
+    pl.semaphore_wait(tp_sem.at[0], len(beside))
+    tell_tp(tp_sem.at[1], (2, n_tp - 2))
     scale = head_dim**-0.5
     rounded = finished.astype(bf16).astype(f32)
     pair_row = iota((PAIR, head_dim), 0)
@@ -387,6 +395,7 @@
             wide_rows[pl.ds(i * out_cols + n, n_mem, stride=own_rows * out_cols), :] = piece
     sums[...] = wide_rows[...].astype(bf16).reshape(n_tp, out_rows * out_cols, head_dim)
 
+    pl.semaphore_wait(tp_sem.at[1], len(beside))
     for d in tp_order:
         to = lax.rem(t + d, n_tp)
         pltpu.make_async_remote_copy(
@@ -481,6 +490,7 @@
         pltpu.SemaphoreType.DMA((16,)),
         pltpu.SemaphoreType.DMA((7,)),
         pltpu.SemaphoreType.DMA((7,)),
+        pltpu.SemaphoreType.REGULAR((2,)),
     ]
     return pl.pallas_call(
         functools.partial(kernel, n_grp, n_tp, n_mem),

time: 39.4 us -> 38.5 us (0.977)
  Pallas kernels: 38.6 us -> 37.8 us
    pallas_call x1, Pallas kernels: 38.6 us -> 37.8 us  [per_device(): pl.pallas_call(functools.partial(kernel, n_grp, n_tp, n_mem), out_shape=p...]
where the time goes in v5:
time: 38.5 us; the launch traced here: 38.4 us
  Pallas kernels  37.8 us (98%)
  local copies, waits for them, and re-layouts  0.62 us (2%)
    pallas_call x1, Pallas kernels, per_device(): pl.pallas_call(functools.partial(kernel, n_grp, n_tp, n_mem), out_shape=p...  37.8 us

profile of v5, /device:TPU:1, one launch (start us, length us, event | category | flops | bytes accessed | tf_op | source)
XLA Modules:
  0.0 38.4 jit_solution(5762397804711967792)
XLA Ops:
  0.0 37.8 %shard_map.109 = bf16[16,1536]{1,0:T(8,128)(2,1)S(1)} custom-call(bf16[16,1536]{1,0:T(8,128)(2,1)} %tokens.1, f32[1536]{0:T(1024)} %gain.1, bf16[1536,1536]{1,0:T(8,128)(2,1)} %w_query.1, bf16[2,1536,128]{2,1,0:T(8,128)(2,1)} %w_keyval.1, bf16[1536,1536]{1,0:T(8,128)(2,1)} %w_out.1, bf16[1,32,128,128]{3,2,1,0:T(8,128)(2,1)} %key_cache.1, ...), custom_call_target="tpu_custom_call" | custom-call | flops 200000000 | bytes 12600000 | tf_op jit(solution)/shard_map/pallas_call | solution.py:495
  37.8 0.6 %copy.13 = bf16[16,1536]{1,0:T(8,128)(2,1)} copy(bf16[16,1536]{1,0:T(8,128)(2,1)S(1)} %shard_map.109) | data formatting | bytes 98304

commit v6 on v5

--- a/solution.py
+++ b/solution.py
@@ -47,7 +47,7 @@
     tokens, gain, w_query, w_keyval, w_out, key_cache, value_cache, req_len, span_request, span_first, new_slot,
     out,
     tok_v, gain_v, wq_v, wkv_v, wo_v, key_v, val_v, len_s, req_s, first_s, lim_s, pair_s, odd_s,
-    part, part_in, table, pick, pick_stat, col_req, leader, qrows, newest, new_score, values, maxima, totals, factors, spans,
+    part, part_in, table, pick, pick_stat, col_req, leader, qrows, key_t, newest, new_score, values, maxima, totals, factors, spans,
     soft_out, soft_in, stat_out, stat_in, blend, att, att_wide, wide_rows, sums, sums_in, done, local_sem, send_sem, recv_sem, tp_sem,
 ):
     g, t, m = lax.axis_index("grp"), lax.axis_index("tp"), lax.axis_index("mem")
@@ -255,6 +255,12 @@
     fresh = jnp.sum(in_pair(rounded) * new_key, axis=1, keepdims=True) * scale
     new_score[...] = jnp.sum(jnp.where(pair_diagonal, fresh, 0.0), axis=0, keepdims=True)
     key_copy.wait()
+
+    def turn(c, carry):
+        key_t[c] = key_v[0, c].T
+        return carry
+
+    lax.fori_loop(0, spans_here, turn, 0)
     val_copy.wait()
     wait_for(qrows, owners - 1, recv_sem.at[1])
 
@@ -279,7 +285,7 @@
 
     all_spans = range(spans_here)
     raws = [
-        lax.dot_general(query_of(c), key_v[0, c], (((1,), (1,)), ((), ())), preferred_element_type=f32)
+        jnp.dot(query_of(c), key_t[c], preferred_element_type=f32)
         for c in all_spans
     ]
     softened = [soften(c, raws[c]) for c in all_spans]
@@ -294,6 +300,17 @@
         request_top = jnp.maximum(request_top, jnp.where(col_req[...] == req_s[c], every[c : c + 1], very_low))
     factor = jnp.exp(every - request_top)
     factors[...] = factor
+    def weigh(c):
+        factor = jnp.sum(jnp.where(diagonal, factors[pl.ds(c, 1), :], 0.0), axis=1, keepdims=True)
+        result = (values[c] * factor).astype(bf16)
+
+        def store():
+            spans[pl.ds(pl.multiple_of(c * SLOTS, SLOTS), SLOTS), :] = result
+
+        return store
+
+    chunks(spans_here, 32, weigh)
+
     group = lane // SLOTS
     said = jnp.where(lax.rem(group, 2) == 0, request_top * leader[...], factor * totals[...])
     high = said.astype(bf16)
@@ -318,17 +335,6 @@
             device_id_type=MESH,
         ).start()
     stat_in[owner] = stat_out[owner]
-
-    def weigh(c):
-        factor = jnp.sum(jnp.where(diagonal, factors[pl.ds(c, 1), :], 0.0), axis=1, keepdims=True)
-        result = (values[c] * factor).astype(bf16)
-
-        def store():
-            spans[pl.ds(pl.multiple_of(c * SLOTS, SLOTS), SLOTS), :] = result
-
-        return store
-
-    chunks(spans_here, 32, weigh)
 
     for dg in far_first(n_grp, 1):
         group_of = lax.rem(g + dg, n_grp)
@@ -469,6 +475,7 @@
         pltpu.VMEM((spans_here, head_dim), jnp.int32),
         pltpu.VMEM((spans_here, head_dim), f32),
         pltpu.VMEM((owners, PAIR, head_dim), bf16),
+        pltpu.VMEM((spans_here, head_dim, key_cache.shape[2]), bf16),
         pltpu.VMEM((PAIR, head_dim), f32),
         pltpu.VMEM((1, head_dim), f32),
         pltpu.VMEM((spans_here, SLOTS, head_dim), f32),

time: 38.5 us -> 38 us (0.987)
  Pallas kernels: 37.8 us -> 37.3 us
    pallas_call x1, Pallas kernels: 37.8 us -> 37.3 us  [per_device(): pl.pallas_call(functools.partial(kernel, n_grp, n_tp, n_mem), out_shape=p...]
where the time goes in v6:
time: 38 us; the launch traced here: 37.9 us
  Pallas kernels  37.3 us (98%)
  local copies, waits for them, and re-layouts  0.62 us (2%)
    pallas_call x1, Pallas kernels, per_device(): pl.pallas_call(functools.partial(kernel, n_grp, n_tp, n_mem), out_shape=p...  37.3 us

profile of v6, /device:TPU:1, one launch (start us, length us, event | category | flops | bytes accessed | tf_op | source)
XLA Modules:
  0.0 37.9 jit_solution(8934227744089109436)
XLA Ops:
  0.0 37.3 %shard_map.109 = bf16[16,1536]{1,0:T(8,128)(2,1)S(1)} custom-call(bf16[16,1536]{1,0:T(8,128)(2,1)} %tokens.1, f32[1536]{0:T(1024)} %gain.1, bf16[1536,1536]{1,0:T(8,128)(2,1)} %w_query.1, bf16[2,1536,128]{2,1,0:T(8,128)(2,1)} %w_keyval.1, bf16[1536,1536]{1,0:T(8,128)(2,1)} %w_out.1, bf16[1,32,128,128]{3,2,1,0:T(8,128)(2,1)} %key_cache.1, ...), custom_call_target="tpu_custom_call" | custom-call | flops 200000000 | bytes 12600000 | tf_op jit(solution)/shard_map/pallas_call | solution.py:502
  37.3 0.6 %copy.13 = bf16[16,1536]{1,0:T(8,128)(2,1)} copy(bf16[16,1536]{1,0:T(8,128)(2,1)S(1)} %shard_map.109) | data formatting | bytes 98304

commit v7 on v6

--- a/solution.py
+++ b/solution.py
@@ -48,7 +48,7 @@
     out,
     tok_v, gain_v, wq_v, wkv_v, wo_v, key_v, val_v, len_s, req_s, first_s, lim_s, pair_s, odd_s,
     part, part_in, table, pick, pick_stat, col_req, leader, qrows, key_t, newest, new_score, values, maxima, totals, factors, spans,
-    soft_out, soft_in, stat_out, stat_in, blend, att, att_wide, wide_rows, sums, sums_in, done, local_sem, send_sem, recv_sem, tp_sem,
+    soft_out, soft_in, stat_out, stat_in, blend, shares, att, att_wide, wide_rows, sums, sums_in, done, local_sem, send_sem, recv_sem, tp_sem,
 ):
     g, t, m = lax.axis_index("grp"), lax.axis_index("tp"), lax.axis_index("mem")
     owners = n_grp * n_mem
@@ -82,11 +82,6 @@
         )
         for c in range(k_chunks)
     ]
-    tok_copy.start()
-    gain_copy.start()
-    for copy in wq_copies + [wkv_copy] + small:
-        copy.start()
-
     barrier = pltpu.get_barrier_semaphore()
 
     def owner_at(dg, dm):
@@ -113,11 +108,18 @@
         key=lambda d: -hops(d[0], n_grp) - hops(d[1] // 2, n_mem // 2),
     )
 
+    tok_copy.start()
+    gain_copy.start()
+    for copy in [wkv_copy] + wq_copies + small:
+        copy.start()
+
     tok_copy.wait()
     gain_copy.wait()
     wide = tok_v[...].astype(f32)
     square = jnp.sum(wide * wide, axis=1, keepdims=True)
     scaled = (wide * gain_v[...].reshape(1, width)).astype(bf16)
+    wkv_copy.wait()
+    new_part = [jnp.dot(scaled, wkv_v[i], preferred_element_type=f32) for i in range(2)]
     projected = jnp.zeros((rows, q_cols), f32)
     for c in range(k_chunks):
         wq_copies[c].wait()
@@ -126,10 +128,8 @@
             wq_v[c * k_step : (c + 1) * k_step, :],
             preferred_element_type=f32,
         )
-    wkv_copy.wait()
     for copy in (key_copy, val_copy, out_copy):
         copy.start()
-    new_part = [jnp.dot(scaled, wkv_v[i], preferred_element_type=f32) for i in range(2)]
     pieces = [projected[:, h * head_dim : (h + 1) * head_dim] for h in range(heads)] + new_part
     pieces += [jnp.broadcast_to(square, (rows, head_dim))]
     pieces += [jnp.zeros((rows, head_dim), f32)] * (SLOTS - len(pieces))
@@ -167,6 +167,51 @@
     table[0] = cosine
     table[1] = jnp.where(lane < half, -sine, sine)
 
+
+    def wait_for(buffer, amount, kind):
+        ref = buffer.at[pl.ds(0, amount)]
+        pltpu.make_async_copy(ref, ref, kind).wait()
+
+    wait_for(part_in, n_mem - 1, recv_sem.at[0])
+    total = part_in[0]
+    for i in range(1, n_mem):
+        total = total + part_in[i]
+    normed = []
+    for i in range(own_rows):
+        block = total[i * SLOTS : (i + 1) * SLOTS]
+        root_mean = jnp.sqrt(block[heads + 2 : heads + 3] / D + epsilon)
+        normed.append(block / root_mean)
+    normed = jnp.concatenate(normed, axis=0)
+    finished = normed * table[0] + pltpu.roll(normed, half, axis=1) * table[1]
+
+    def in_pair(block):
+        sub_row = iota((8, head_dim), 0)
+        middle = jnp.where(sub_row < 4, block[8:16], pltpu.roll(block[24:32], 4, axis=0))
+        return jnp.concatenate([block[0:8], middle, block[16:24]], axis=0)
+
+    qrows[owner] = in_pair(finished).astype(bf16)
+
+    for d in owner_order:
+        pltpu.make_async_remote_copy(
+            src_ref=qrows.at[owner],
+            dst_ref=qrows.at[owner],
+            send_sem=send_sem.at[1],
+            recv_sem=recv_sem.at[1],
+            device_id=owner_at(*d)[1],
+            device_id_type=MESH,
+        ).start()
+    pl.semaphore_wait(tp_sem.at[0], len(beside))
+    tell_tp(tp_sem.at[1], (2, n_tp - 2))
+    scale = head_dim**-0.5
+    rounded = finished.astype(bf16).astype(f32)
+    pair_row = iota((PAIR, head_dim), 0)
+    pair_lane = iota((PAIR, head_dim), 1)
+    of_first = pair_row < 12
+    pair_diagonal = pair_lane == jnp.where(of_first, pair_row, jnp.where(pair_row < 16, pair_row + 32, pair_row + 16))
+    new_key = jnp.where(of_first, rounded[heads : heads + 1], rounded[SLOTS + heads : SLOTS + heads + 1])
+    newest[...] = jnp.where(of_first, rounded[heads + 1 : heads + 2], rounded[SLOTS + heads + 1 : SLOTS + heads + 2])
+    fresh = jnp.sum(in_pair(rounded) * new_key, axis=1, keepdims=True) * scale
+    new_score[...] = jnp.sum(jnp.where(pair_diagonal, fresh, 0.0), axis=0, keepdims=True)
     def span_scalars(c, carry):
         r = jnp.maximum(req_s[c], 0)
         lim_s[c] = jnp.where(req_s[c] >= 0, len_s[r] - first_s[c], 0)
@@ -210,50 +255,6 @@
     wanted = iota((owners, 6 * spans_here), 0) * 2 + stat_column // (3 * spans_here)
     pick_stat[...] = jnp.where(wanted == by_stat, 1.0, 0.0).astype(bf16)
 
-    def wait_for(buffer, amount, kind):
-        ref = buffer.at[pl.ds(0, amount)]
-        pltpu.make_async_copy(ref, ref, kind).wait()
-
-    wait_for(part_in, n_mem - 1, recv_sem.at[0])
-    total = part_in[0]
-    for i in range(1, n_mem):
-        total = total + part_in[i]
-    normed = []
-    for i in range(own_rows):
-        block = total[i * SLOTS : (i + 1) * SLOTS]
-        root_mean = jnp.sqrt(block[heads + 2 : heads + 3] / D + epsilon)
-        normed.append(block / root_mean)
-    normed = jnp.concatenate(normed, axis=0)
-    finished = normed * table[0] + pltpu.roll(normed, half, axis=1) * table[1]
-
-    def in_pair(block):
-        sub_row = iota((8, head_dim), 0)
-        middle = jnp.where(sub_row < 4, block[8:16], pltpu.roll(block[24:32], 4, axis=0))
-        return jnp.concatenate([block[0:8], middle, block[16:24]], axis=0)
-
-    qrows[owner] = in_pair(finished).astype(bf16)
-
-    for d in owner_order:
-        pltpu.make_async_remote_copy(
-            src_ref=qrows.at[owner],
-            dst_ref=qrows.at[owner],
-            send_sem=send_sem.at[1],
-            recv_sem=recv_sem.at[1],
-            device_id=owner_at(*d)[1],
-            device_id_type=MESH,
-        ).start()
-    pl.semaphore_wait(tp_sem.at[0], len(beside))
-    tell_tp(tp_sem.at[1], (2, n_tp - 2))
-    scale = head_dim**-0.5
-    rounded = finished.astype(bf16).astype(f32)
-    pair_row = iota((PAIR, head_dim), 0)
-    pair_lane = iota((PAIR, head_dim), 1)
-    of_first = pair_row < 12
-    pair_diagonal = pair_lane == jnp.where(of_first, pair_row, jnp.where(pair_row < 16, pair_row + 32, pair_row + 16))
-    new_key = jnp.where(of_first, rounded[heads : heads + 1], rounded[SLOTS + heads : SLOTS + heads + 1])
-    newest[...] = jnp.where(of_first, rounded[heads + 1 : heads + 2], rounded[SLOTS + heads + 1 : SLOTS + heads + 2])
-    fresh = jnp.sum(in_pair(rounded) * new_key, axis=1, keepdims=True) * scale
-    new_score[...] = jnp.sum(jnp.where(pair_diagonal, fresh, 0.0), axis=0, keepdims=True)
     key_copy.wait()
 
     def turn(c, carry):
@@ -363,13 +364,21 @@
     whole = jnp.sum(factor * total, axis=0, keepdims=True) + new_factor
     blend[...] = factor / whole
     new_share = jnp.sum(jnp.where(pair_diagonal, new_factor / whole, 0.0), axis=1, keepdims=True)
+
+    def spread(b, carry):
+        for u in range(16):
+            s = b * 16 + u
+            share = jnp.sum(jnp.where(pair_diagonal, blend[pl.ds(s, 1), :], 0.0), axis=1, keepdims=True)
+            shares[s] = jnp.broadcast_to(share, (PAIR, head_dim))
+        return carry
+
+    lax.fori_loop(0, owners // 16, spread, 0)
     wait_for(soft_in, owners - 1, recv_sem.at[2])
 
     def join(b, carry):
         for u in range(16):
             s = b * 16 + u
-            share = jnp.sum(jnp.where(pair_diagonal, blend[pl.ds(s, 1), :], 0.0), axis=1, keepdims=True)
-            carry = carry + share * soft_in[s].astype(f32)
+            carry = carry + shares[s] * soft_in[s].astype(f32)
         return carry
 
     att[m] = lax.fori_loop(0, owners // 16, join, new_share * newest[...]).astype(bf16)
@@ -387,7 +396,7 @@
     wait_for(att, n_mem - 1, recv_sem.at[3])
 
     out_cols = wo_v.shape[1] // head_dim
-    att_wide[...] = att[...].astype(f32).reshape(n_mem * PAIR, head_dim)
+    att_wide[0 : n_mem * PAIR, :] = att[...].astype(f32).reshape(n_mem * PAIR, head_dim)
 
     def head_rows(h):
         second = h + 16 if h < 8 else h + 4
@@ -399,7 +408,7 @@
         for i in range(own_rows):
             piece = product[i * n_mem : (i + 1) * n_mem, n * head_dim : (n + 1) * head_dim]
             wide_rows[pl.ds(i * out_cols + n, n_mem, stride=own_rows * out_cols), :] = piece
-    sums[...] = wide_rows[...].astype(bf16).reshape(n_tp, out_rows * out_cols, head_dim)
+    sums[...] = wide_rows[0 : rows * out_cols, :].astype(bf16).reshape(n_tp, out_rows * out_cols, head_dim)
 
     pl.semaphore_wait(tp_sem.at[1], len(beside))
     for d in tp_order:
@@ -428,7 +437,7 @@
             device_id_type=MESH,
         ).start()
     wait_for(done, n_tp - 1, recv_sem.at[5])
-    wide_rows[...] = done[...].astype(f32).reshape(rows * out_cols, head_dim)
+    wide_rows[0 : rows * out_cols, :] = done[...].astype(f32).reshape(rows * out_cols, head_dim)
     for n in range(out_cols):
         out[:, n * head_dim : (n + 1) * head_dim] = wide_rows[pl.ds(n, rows, stride=out_cols), :].astype(bf16)
 
@@ -467,7 +476,7 @@
         pltpu.SMEM((spans_here,), jnp.int32),
         pltpu.SMEM((spans_here,), jnp.int32),
         pltpu.SMEM((spans_here,), jnp.int32),
-        pltpu.VMEM((rows * SLOTS, head_dim), f32),
+        pltpu.VMEM((rows * SLOTS + SLOTS, head_dim), f32),
         pltpu.VMEM((n_mem, tile, head_dim), f32),
         pltpu.VMEM((2, tile, head_dim), f32),
         pltpu.VMEM((owners * PAIR, spans_here * SLOTS), bf16),
@@ -488,9 +497,10 @@
         pltpu.VMEM((owners, 1, head_dim), f32),
         pltpu.VMEM((owners, 1, head_dim), f32),
         pltpu.VMEM((owners, head_dim), f32),
+        pltpu.VMEM((owners, PAIR, head_dim), f32),
         pltpu.VMEM((n_mem, PAIR, head_dim), bf16),
-        pltpu.VMEM((n_mem * PAIR, head_dim), f32),
-        pltpu.VMEM((n_tp * slab, head_dim), f32),
+        pltpu.VMEM((n_mem * PAIR + PAIR, head_dim), f32),
+        pltpu.VMEM((n_tp * slab + slab, head_dim), f32),
         pltpu.VMEM((n_tp, slab, head_dim), bf16),
         pltpu.VMEM((n_tp, slab, head_dim), bf16),
         pltpu.VMEM((n_tp, slab, head_dim), bf16),

time: 38 us -> 37.7 us (level)
  no operation moved by 1% of the time
where the time goes in v7:
time: 37.7 us; the launch traced here: 37.6 us
  Pallas kernels  37 us (98%)
  local copies, waits for them, and re-layouts  0.62 us (2%)
    pallas_call x1, Pallas kernels, per_device(): pl.pallas_call(functools.partial(kernel, n_grp, n_tp, n_mem), out_shape=p...  37 us

profile of v7, /device:TPU:1, one launch (start us, length us, event | category | flops | bytes accessed | tf_op | source)
XLA Modules:
  0.0 37.6 jit_solution(9956722344996077259)
XLA Ops:
  0.0 37.0 %shard_map.109 = bf16[16,1536]{1,0:T(8,128)(2,1)S(1)} custom-call(bf16[16,1536]{1,0:T(8,128)(2,1)} %tokens.1, f32[1536]{0:T(1024)} %gain.1, bf16[1536,1536]{1,0:T(8,128)(2,1)} %w_query.1, bf16[2,1536,128]{2,1,0:T(8,128)(2,1)} %w_keyval.1, bf16[1536,1536]{1,0:T(8,128)(2,1)} %w_out.1, bf16[1,32,128,128]{3,2,1,0:T(8,128)(2,1)} %key_cache.1, ...), custom_call_target="tpu_custom_call" | custom-call | flops 200000000 | bytes 12600000 | tf_op jit(solution)/shard_map/pallas_call | solution.py:512
  37.0 0.6 %copy.13 = bf16[16,1536]{1,0:T(8,128)(2,1)} copy(bf16[16,1536]{1,0:T(8,128)(2,1)S(1)} %shard_map.109) | data formatting | bytes 98304

commit v8 on v7

--- a/solution.py
+++ b/solution.py
@@ -47,7 +47,7 @@
     tokens, gain, w_query, w_keyval, w_out, key_cache, value_cache, req_len, span_request, span_first, new_slot,
     out,
     tok_v, gain_v, wq_v, wkv_v, wo_v, key_v, val_v, len_s, req_s, first_s, lim_s, pair_s, odd_s,
-    part, part_in, table, pick, pick_stat, col_req, leader, qrows, key_t, newest, new_score, values, maxima, totals, factors, spans,
+    part, part_in, table, pick, pick_stat, same, leader, qrows, key_t, newest, new_score, values, maxima, totals, factors, spans,
     soft_out, soft_in, stat_out, stat_in, blend, shares, att, att_wide, wide_rows, sums, sums_in, done, local_sem, send_sem, recv_sem, tp_sem,
 ):
     g, t, m = lax.axis_index("grp"), lax.axis_index("tp"), lax.axis_index("mem")
@@ -232,11 +232,12 @@
         by_column = jnp.where(column // SLOTS == c, req_s[c], by_column)
         by_row = jnp.where(in_rows == c, req_s[c], by_row)
         by_stat = jnp.where(lax.rem(stat_column, spans_here) == c, req_s[c], by_stat)
-    col_req[...] = by_row
     first_of = jnp.ones((spans_here, head_dim), f32)
     for c in range(spans_here):
         first_of = jnp.where((by_row == req_s[c]) & (in_rows > c), 0.0, first_of)
     leader[...] = first_of
+    for c in range(spans_here):
+        same[c] = jnp.where(by_row == req_s[c], 0.0, very_low * 1e5)
     row_in = lax.rem(column, SLOTS)
     nowhere = -requests * SLOTS
     of_first = jnp.where(row_in < 12, row_in, nowhere)
@@ -298,7 +299,7 @@
     every = maxima[...]
     request_top = every
     for c in range(spans_here):
-        request_top = jnp.maximum(request_top, jnp.where(col_req[...] == req_s[c], every[c : c + 1], very_low))
+        request_top = jnp.maximum(request_top, every[c : c + 1] + same[c])
     factor = jnp.exp(every - request_top)
     factors[...] = factor
     def weigh(c):
@@ -481,7 +482,7 @@
         pltpu.VMEM((2, tile, head_dim), f32),
         pltpu.VMEM((owners * PAIR, spans_here * SLOTS), bf16),
         pltpu.VMEM((owners, 6 * spans_here), bf16),
-        pltpu.VMEM((spans_here, head_dim), jnp.int32),
+        pltpu.VMEM((spans_here, spans_here, head_dim), f32),
         pltpu.VMEM((spans_here, head_dim), f32),
         pltpu.VMEM((owners, PAIR, head_dim), bf16),
         pltpu.VMEM((spans_here, head_dim, key_cache.shape[2]), bf16),

time: 37.7 us -> 37.7 us (level)
  no operation moved by 1% of the time
where the time goes in v8:
time: 37.7 us; the launch traced here: 37.6 us
  Pallas kernels  37 us (98%)
  local copies, waits for them, and re-layouts  0.62 us (2%)
    pallas_call x1, Pallas kernels, per_device(): pl.pallas_call(functools.partial(kernel, n_grp, n_tp, n_mem), out_shape=p...  37 us

profile of v8, /device:TPU:1, one launch (start us, length us, event | category | flops | bytes accessed | tf_op | source)
XLA Modules:
  0.0 37.6 jit_solution(12109454949707330337)
XLA Ops:
  0.0 37.0 %shard_map.109 = bf16[16,1536]{1,0:T(8,128)(2,1)S(1)} custom-call(bf16[16,1536]{1,0:T(8,128)(2,1)} %tokens.1, f32[1536]{0:T(1024)} %gain.1, bf16[1536,1536]{1,0:T(8,128)(2,1)} %w_query.1, bf16[2,1536,128]{2,1,0:T(8,128)(2,1)} %w_keyval.1, bf16[1536,1536]{1,0:T(8,128)(2,1)} %w_out.1, bf16[1,32,128,128]{3,2,1,0:T(8,128)(2,1)} %key_cache.1, ...), custom_call_target="tpu_custom_call" | custom-call | flops 200000000 | bytes 12600000 | tf_op jit(solution)/shard_map/pallas_call | solution.py:513
  37.0 0.6 %copy.13 = bf16[16,1536]{1,0:T(8,128)(2,1)} copy(bf16[16,1536]{1,0:T(8,128)(2,1)S(1)} %shard_map.109) | data formatting | bytes 98304
